TPU v7x, 256 devices: a whole 4x4x8 slice. The times are simulated.
256 devices in a mesh: user: 32 (over z, y_lo, core), item: 8 (over y_hi, x).
Axes of the slice: x: 4, y: 4 (y_hi: 2, y_lo: 2; y = y_hi * 2 + y_lo), z: 8, core: 2. Of those that a mesh axis runs over, the one named last changes fastest.
Arguments:
- user_factors: bfloat16 [32768, 128], P('user'), may hold values from -1.796875 to 1.796875
- item_factors: bfloat16 [8192, 128], P('item'), may hold values from -1.796875 to 1.796875
- block_user: int32 [32, 8, 128], P('user', 'item'), may hold values from 0 to 255
- block_item: int32 [32, 8, 128], P('user', 'item'), may hold values from 0 to 7
- live_blocks: int32 [32, 8], P('user', 'item'), may hold values from 16 to 128, as said below
- ratings: int32 [32, 8, 128, 128, 128], P('user', 'item'), may hold values from 0 to 5
Outputs:
- new_users: float32 [32768, 128], P('user')
- new_items: float32 [8192, 128], P('item')
Inputs may be any that keep to these rules, and one draw needn't show every extreme that they name: `live_blocks`: one device uses all 128 slots in every draw.
All inputs are finite; a program needn't handle non-finite values.
Results may differ from a plain program's by a relative error of at most 0.00091.
Values may be sent and summed in bfloat16 or wider, within the bound.
A program may use at most 128 MiB of HBM per device.

v0:
```python
import jax
import jax.numpy as jnp
from jax import lax
from jax.sharding import PartitionSpec as P

user_step = 0.1
item_step = 0.04
shrinkage = 0.1


def body(user_factors, item_factors, block_user, block_item, live_blocks, ratings):
    tile_edge = ratings.shape[-1]
    slot_count = ratings.shape[2]
    factor_dim = user_factors.shape[1]
    local_rows = user_factors.shape[0]
    item_count = item_factors.shape[0] // tile_edge
    user_block = block_user.reshape(slot_count)
    item_block = block_item.reshape(slot_count)
    everyone = lax.all_gather(user_factors, "user", axis=0, tiled=True)
    user_tiles = everyone.reshape(-1, tile_edge, factor_dim)[user_block]
    item_tiles = item_factors.reshape(-1, tile_edge, factor_dim)[item_block]
    predicted = jnp.einsum(
        "bir,bjr->bij", user_tiles, item_tiles, preferred_element_type=jnp.float32
    )
    scores = ratings.reshape(slot_count, tile_edge, tile_edge)
    slots = jnp.arange(slot_count, dtype=jnp.int32) < live_blocks.reshape(())
    observed = (scores > 0) & slots[:, None, None]
    target = scores.astype(jnp.float32) - 3.0
    errors = jnp.where(observed, predicted - target, jnp.float32(0.0)).astype(jnp.bfloat16)
    user_terms = jnp.einsum("bij,bjr->bir", errors, item_tiles, preferred_element_type=jnp.float32)
    item_terms = jnp.einsum("bij,bir->bjr", errors, user_tiles, preferred_element_type=jnp.float32)
    picked = local_rows * lax.axis_size("user") // tile_edge
    selector = (user_block[:, None] == jnp.arange(picked, dtype=jnp.int32)[None, :]).astype(
        jnp.float32
    )
    summed = jnp.einsum("bs,bir->sir", selector, user_terms, precision=lax.Precision.HIGHEST)
    user_grad = lax.psum_scatter(
        summed.reshape(local_rows * lax.axis_size("user"), factor_dim),
        "user",
        scatter_dimension=0,
        tiled=True,
    )
    user_grad = lax.psum(user_grad, "item")
    item_selector = (
        item_block[:, None] == jnp.arange(item_count, dtype=jnp.int32)[None, :]
    ).astype(jnp.float32)
    item_local = jnp.einsum(
        "bs,bjr->sjr", item_selector, item_terms, precision=lax.Precision.HIGHEST
    )
    item_grad = lax.psum(item_local.reshape(-1, factor_dim), "user")
    user_now = user_factors.astype(jnp.float32)
    item_now = item_factors.astype(jnp.float32)
    new_users = user_now - user_step * (user_grad + shrinkage * user_now)
    new_items = item_now - item_step * (item_grad + shrinkage * item_now)
    return (new_users, new_items)


def solution(mesh):
    return jax.shard_map(
        body,
        mesh=mesh,
        in_specs=(
            P("user", None),
            P("item", None),
            P("user", "item", None),
            P("user", "item", None),
            P("user", "item"),
            P("user", "item", None, None, None),
        ),
        out_specs=(P("user", None), P("item", None)),
        check_vma=False,
    )
```

profile of v0, /device:TPU:6, one launch (start us, length us, event | category | flops | bytes accessed | tf_op | source)
XLA Modules:
  0.0 660.0 jit_solution(4696215486198264600)
XLA Ops:
  7.2 0.0 all-gather.2.cloned.1.call-start
  7.2 0.7 all-gather.2.cloned.1.call-update
  7.9 0.0 reduce-scatter.2.cloned.1.call-start
  8.6 0.7 fusion.17
  9.3 4.0 gather_fusion.1
  13.3 0.0 copy-done.4
  13.3 71.8 %all-gather.2.cloned.1.call-done = bf16[32768,128]{1,0:T(8,128)(2,1)} async-done(((bf16[1024,128]{1,0:T(8,128)(2,1)}), bf16[32768,128]{1,0:T(8,128)(2,1)}) %all-gather.2.cloned.1.call-update) | async-done | bytes 8388624 | tf_op jit(solution)/shard_map/all_gather | solution.py:19
  85.1 6.4 gather_fusion
  91.5 11.5 %fusion.1 = bf16[128,128,128]{2,1,0:T(8,128)(2,1)S(1)} fusion(s32[1,1,128,128,128]{4,3,2,1,0:T(8,128)} %param.11, pred[128]{0:T(512)(128)(4,1)S(1)} %iota_compare_fusion.2, bf16[128,128,128]{2,1,0:T(8,128)(2,1)} %gather_fusion, bf16[128,128,128]{2,1,0:T(8,128)(2,1)} %gather_fusion.1), kind=kOutput, calls=%fused_computation.4 | convolution fusion | flops 551550976 | bytes 20971648 | tf_op jit(solution)/shard_map/bir,bjr->bij/dot_general | solution.py:22
  103.0 0.0 copy-done.1
  103.0 0.0 copy-start.2
  103.0 4.5 fusion.18
  107.5 0.0 copy-done.2
  107.5 15.5 %fusion.4 = f32[256,128,128]{2,0,1:T(8,128)S(1)} fusion(f32[128,128,128]{2,1,0:T(8,128)} %fusion.18, s32[128]{0:T(128)S(1)} %bitcast.42), kind=kOutput, calls=%fused_computation.7 | convolution fusion | flops 6442483712 | bytes 25166336 | tf_op jit(solution)/shard_map/bs,bir->sir/dot_general | solution.py:36
  123.1 20.0 %copy.8 = f32[256,128,128]{2,1,0:T(8,128)} copy(f32[256,128,128]{2,0,1:T(8,128)S(1)} %fusion.4) | data formatting | bytes 33554432 | tf_op jit(solution)/shard_map/bs,bir->sir/dot_general | solution.py:36
  143.1 0.0 reduce-scatter.2.cloned.1.call-update
  143.1 0.0 copy-start.5
  143.1 0.3 all-reduce.5.cloned.1.call-start
  143.4 5.0 fusion.19
  148.4 0.0 copy-done.5
  148.4 0.0 copy-start
  148.4 0.0 copy-start.3
  148.5 7.5 %fusion.2 = f32[8,128,128]{2,0,1:T(8,128)S(1)} fusion(f32[128,128,128]{2,1,0:T(8,128)S(1)} %fusion.19, s32[128]{0:T(128)S(1)} %bitcast.43), kind=kOutput, calls=%fused_computation.5 | convolution fusion | flops 201327616 | bytes 8913408 | tf_op jit(solution)/shard_map/bs,bjr->sjr/dot_general | solution.py:47
  156.0 0.9 copy.9
  156.8 0.0 all-reduce.5.cloned.1.call-update
  156.9 0.0 all-reduce.3.cloned.1.call-start
  156.9 173.3 %reduce-scatter.2.cloned.1.call-done = f32[1024,128]{1,0:T(8,128)} async-done(((f32[32768,128]{1,0:T(8,128)}), f32[1024,128]{1,0:T(8,128)}) %reduce-scatter.2.cloned.1.call-update) | async-done | bytes 524304 | tf_op jit(solution)/shard_map/reduce_scatter | solution.py:37
  330.2 0.0 all-reduce.3.cloned.1.call-update
  330.3 229.6 %all-reduce.5.cloned.1.call-done = f32[1024,128]{1,0:T(8,128)} async-done(((f32[1024,128]{1,0:T(8,128)}), f32[1024,128]{1,0:T(8,128)}) %all-reduce.5.cloned.1.call-update) | async-done | bytes 524304 | tf_op jit(solution)/shard_map/psum | solution.py:50
  559.9 1.9 convert_subtract_fusion
  561.8 89.8 %all-reduce.3.cloned.1.call-done = f32[1024,128]{1,0:T(8,128)} async-done(((f32[1024,128]{1,0:T(8,128)}), f32[1024,128]{1,0:T(8,128)}) %all-reduce.3.cloned.1.call-update) | async-done | bytes 524304 | tf_op jit(solution)/shard_map/psum | solution.py:43
  651.6 1.9 convert_subtract_fusion.1
  (8 shorter events, 0.0 us)
Async XLA Ops:
  7.2 77.9 %all-gather.2.cloned.1.call-start = ((), (), s32[]{:S(2)}) async-start(), calls=%async_computation.1 | async-start | bytes 8650752 | tf_op jit(solution)/shard_map/all_gather | solution.py:19
  7.9 322.3 %reduce-scatter.2.cloned.1.call-start = ((), (), s32[]{:S(2)}) async-start(), calls=%async_computation.2 | async-start | bytes 17301504 | tf_op jit(solution)/shard_map/reduce_scatter | solution.py:37
  9.3 4.0 copy-start.4
  91.5 11.5 %copy-start.1 = (bf16[128,128,128]{2,1,0:T(8,128)(2,1)S(1)}, bf16[128,128,128]{2,1,0:T(8,128)(2,1)}, u32[]{:S(2)}) copy-start(bf16[128,128,128]{2,1,0:T(8,128)(2,1)} %gather_fusion.1) | copy-start | bytes 12582916
  103.0 4.5 copy-start.2
  143.1 5.3 copy-start.5
  143.1 416.7 %all-reduce.5.cloned.1.call-start = ((), (), s32[]{:S(2)}) async-start(), calls=%async_computation.4 | async-start | bytes 1048576 | tf_op jit(solution)/shard_map/psum | solution.py:50
  148.4 411.4 %copy-start = (bf16[1024,128]{1,0:T(8,128)(2,1)S(1)}, bf16[1024,128]{1,0:T(8,128)(2,1)}, u32[]{:S(2)}) copy-start(bf16[1024,128]{1,0:T(8,128)(2,1)} %param.7) | copy-start | bytes 786436
  148.4 503.1 %copy-start.3 = (bf16[1024,128]{1,0:T(8,128)(2,1)S(1)}, bf16[1024,128]{1,0:T(8,128)(2,1)}, u32[]{:S(2)}) copy-start(bf16[1024,128]{1,0:T(8,128)(2,1)} %param.6) | copy-start | bytes 786436
  156.9 494.7 %all-reduce.3.cloned.1.call-start = ((), (), s32[]{:S(2)}) async-start(), calls=%async_computation.3 | async-start | bytes 1048576 | tf_op jit(solution)/shard_map/psum | solution.py:43
Sparse Core Ops, SparseCore 0:
  9.9 75.1 all-gather.1
  143.3 186.9 reduce-scatter.1
  333.4 226.3 all-reduce.4
  562.5 88.9 all-reduce.2
where the time goes:
time: 662 us; the launch traced here: 660 us
  waiting for transfers between devices  565 us (85%)
  matrix products  44.1 us (7%)
  local copies, waits for them, and re-layouts  31.4 us (5%)
  between operations  14.5 us (2%)
    psum x1, waiting for transfers between devices, body(): item_grad = lax.psum(item_local.reshape(-1, factor_dim), 'user')  230 us
    reduce_scatter x1, waiting for transfers between devices, body(): lax.psum_scatter(summed.reshape(local_rows * lax.axis_size('user'), facto...  173 us
    psum x1, waiting for transfers between devices, body(): user_grad = lax.psum(user_grad, 'item')  89.8 us
    all_gather x1, waiting for transfers between devices, body(): everyone = lax.all_gather(user_factors, 'user', axis=0, tiled=True)  71.8 us
    dot_general x1, local copies, waits for them, and re-layouts, body(): jnp.einsum('bs,bir->sir', selector, user_terms, precision=lax.Precision.H...  20 us
    dot_general x1, matrix products, body(): jnp.einsum('bs,bir->sir', selector, user_terms, precision=lax.Precision.H...  15.5 us
  transfers between devices with their start and end apart: 4, of which 4 were waited for; matrix products, arithmetic and copies ran while one was open for 3% of the time, Pallas kernels for 0%

commit v1 on v0

v1 whole, which is shorter than its diff:
```python
import functools

import jax
import jax.numpy as jnp
from jax import lax
from jax.experimental import pallas as pl
from jax.experimental.pallas import tpu as pltpu
from jax.sharding import PartitionSpec as P

MESH = pl.DeviceIdType.MESH


def here():
    p = lax.axis_index("user")
    q = lax.axis_index("item")
    return p // 4, lax.rem(p // 2, 2), q // 4, lax.rem(q, 4), lax.rem(p, 2)


def device(z, y, x, c):
    return (z * 4 + lax.rem(y, 2) * 2 + c, (y // 2) * 4 + x)


def neighbours():
    z, ylo, yhi, x, c = here()
    y = yhi * 2 + ylo
    up = lambda v, n: lax.rem(v + 1, n)
    down = lambda v, n: lax.rem(v + n - 1, n)
    return {
        "x": (device(z, y, up(x, 4), c), device(z, y, down(x, 4), c)),
        "y": (device(z, up(y, 4), x, c), device(z, down(y, 4), x, c)),
        "z": (device(up(z, 8), y, x, c), device(down(z, 8), y, x, c)),
        "pair": device(z, yhi * 2 + 1 - ylo, x, c),
        "mate": device(z, y, x, 1 - c),
    }


def meet(near):
    barrier = pltpu.get_barrier_semaphore()
    others = [*near["x"], *near["y"], *near["z"], near["mate"]]
    for other in others:
        pl.semaphore_signal(barrier, inc=1, device_id=other, device_id_type=MESH)
    pl.semaphore_wait(barrier, len(others))


class Sender:
    def __init__(self, send_sems, recv_sems):
        self.send_sems, self.recv_sems, self.used, self.copies = send_sems, recv_sems, 0, []

    def __call__(self, src, dst, where):
        copy = pltpu.make_async_remote_copy(
            src_ref=src,
            dst_ref=dst,
            send_sem=self.send_sems.at[self.used],
            recv_sem=self.recv_sems.at[self.used],
            device_id=where,
            device_id_type=MESH,
        )
        copy.start()
        self.used += 1
        self.copies.append(copy)
        return copy

    def drain(self):
        for copy in self.copies:
            copy.wait_send()


ROWS_A, ROWS_B, ROWS_C = 64, 32, 32
GATHER_COPIES = 160


def gather_kernel(split, own, ratings, lists, users, mate_ratings, mate_lists, local_sem, send_sems, recv_sems):
    z, ylo, yhi, x, c = here()
    y = yhi * 2 + ylo
    near = neighbours()
    keep = pltpu.make_async_copy(own, users.at[z, ylo], local_sem)
    keep.start()
    meet(near)
    send = Sender(send_sems, recv_sems)
    keep.wait()
    rows_a = pl.ds(0, split[0])
    rows_b = pl.ds(split[0], split[1])
    rows_c = pl.ds(split[0] + split[1], split[2])

    def zed(offset):
        return lax.rem(z + offset + 8, 8)

    def part_a(zz, low, xx, half=None):
        if half is None:
            return users.at[zz, low, :, xx, rows_a]
        return users.at[zz, low, half, xx, rows_a]

    def part_b(zz, yy, half=None):
        if half is None:
            return users.at[zz, lax.rem(yy, 2), yy // 2, :, rows_b]
        return users.at[zz, lax.rem(yy, 2), yy // 2, pl.ds(2 * half, 2), rows_b]

    def part_c(zz, low, half=None):
        if half is None:
            return users.at[zz, low, :, :, rows_c]
        return users.at[zz, low, half, :, rows_c]

    parts = {
        "A": lambda zz, half=None: part_a(zz, ylo, x, half),
        "B": lambda zz, half=None: part_b(zz, y, half),
        "C": lambda zz, half=None: part_c(zz, ylo, half),
        "D": lambda zz, half=None: part_c(zz, 1 - ylo, half),
    }
    along_z, pair, first, last = {}, {}, {}, []

    def z_send(name, step):
        for way in (0, 1):
            offset = -(step - 1) if way == 0 else step - 1
            block = parts[name](zed(offset), way if step == 4 else None)
            along_z[name, step, way] = send(block, block, near["z"][way])

    def z_wait(name, step):
        for way in (0, 1):
            along_z[name, step, way].wait_recv()

    def pair_send(offset):
        block = part_a(zed(offset), ylo, x)
        pair[offset] = send(block, block, near["pair"])

    def x_send(offset, low):
        if offset == 0 and low == 0:
            return
        block = part_a(zed(offset), ylo if low == 0 else 1 - ylo, x)
        first["x", offset, low] = [send(block, block, near["x"][way]) for way in (0, 1)]

    def y_send(offset):
        block = part_b(zed(offset), y)
        first["y", offset, 0] = [send(block, block, near["y"][way]) for way in (0, 1)]

    def forward(axis, offset, low):
        zz = zed(offset)
        if axis == "x" and offset == 0 and low == 0:
            return
        for way in (0, 1):
            first[axis, offset, low][way].wait_recv()
            if axis == "y" and offset == 0:
                continue
            back = 3 if way == 0 else 1
            if axis == "x":
                block = part_a(zz, ylo if low == 0 else 1 - ylo, lax.rem(x + back, 4), way)
            else:
                block = part_b(zz, lax.rem(y + back, 4), way)
            last.append(send(block, block, near[axis][way]))

    z_send("A", 1)
    z_send("B", 1)
    pair_c = send(part_c(z, ylo), part_c(z, ylo), near["pair"])
    pair_send(0)
    x_send(0, 0)
    y_send(0)
    z_send("C", 1)
    far = send(ratings, mate_ratings, near["mate"])
    far_lists = send(lists, mate_lists, near["mate"])
    before = [0]
    for step in (1, 2, 3, 4):
        offsets = [-step, step] if step < 4 else [4]
        z_wait("A", step)
        if step < 4:
            z_send("A", step + 1)
        z_wait("B", step)
        if step < 4:
            z_send("B", step + 1)
        for offset in offsets:
            pair_send(offset)
            x_send(offset, 0)
            y_send(offset)
        if step == 1:
            pair_c.wait_recv()
            z_send("D", 1)
        z_wait("C", step)
        if step < 4:
            z_send("C", step + 1)
        for offset in before:
            pair[offset].wait_recv()
            x_send(offset, 1)
        for offset in before:
            forward("y", offset, 0)
            forward("x", offset, 0)
        if step > 1:
            z_wait("D", step - 1)
            z_send("D", step)
            for offset in earlier:
                forward("x", offset, 1)
        earlier, before = before, offsets
    for offset in before:
        pair[offset].wait_recv()
        x_send(offset, 1)
    for offset in before:
        forward("y", offset, 0)
        forward("x", offset, 0)
    for offset in earlier + before:
        forward("x", offset, 1)
    z_wait("D", 4)
    for copy in last:
        copy.wait_recv()
    far.wait_recv()
    far_lists.wait_recv()
    send.drain()


def gather(user_factors, ratings, lists, vmem=True):
    space = pltpu.VMEM if vmem else pltpu.HBM
    return pl.pallas_call(
        functools.partial(gather_kernel, (ROWS_A, ROWS_B, ROWS_C)),
        out_shape=(
            jax.ShapeDtypeStruct((8, 2, 2, 4, 128, 128), jnp.bfloat16),
            jax.ShapeDtypeStruct(ratings.shape, jnp.int32),
            jax.ShapeDtypeStruct(lists.shape, jnp.int32),
        ),
        in_specs=[
            pl.BlockSpec(memory_space=space),
            pl.BlockSpec(memory_space=pltpu.HBM),
            pl.BlockSpec(memory_space=pltpu.VMEM),
        ],
        out_specs=(
            pl.BlockSpec(memory_space=space),
            pl.BlockSpec(memory_space=pltpu.HBM),
            pl.BlockSpec(memory_space=pltpu.VMEM),
        ),
        scratch_shapes=[
            pltpu.SemaphoreType.DMA,
            pltpu.SemaphoreType.DMA((GATHER_COPIES,)),
            pltpu.SemaphoreType.DMA((GATHER_COPIES,)),
        ],
        compiler_params=pltpu.CompilerParams(
            collective_id=0, has_side_effects=True, vmem_limit_bytes=40 * 2**20
        ),
    )(user_factors.reshape(2, 4, 128, 128), ratings, lists)


GROUP = 4
SLOTS = 32


def local_kernel(core, lists, mate_lists, users_hbm, items, ratings, mate_ratings, user_out, item_out, users, user_sum, item_sum, stack, order, users_sem, rating_sems, out_sems):
    load = pltpu.make_async_copy(users_hbm, users, users_sem)
    load.start()
    mine = core[0]
    edge = ratings.shape[1]

    def scan(table, base):
        def visit(slot, count):
            block = table[0, slot]
            item = table[1, slot]
            order[count] = (((base + slot) * 256 + block) * 8) + item
            keep = lax.rem(block // 8, 2) == mine
            return count + keep.astype(jnp.int32)
        return visit

    count = lax.fori_loop(0, lists[2, 0], scan(lists, 0), jnp.int32(0))
    count = lax.fori_loop(0, mate_lists[2, 0], scan(mate_lists, 128), count)
    groups = (count + GROUP - 1) // GROUP
    for k in range(GROUP):
        order[count + k] = 0

    def fetch(n, start):
        slot = order[n] // 2048
        place = lax.rem(n, SLOTS)

        @pl.when(slot < 128)
        def _():
            copy = pltpu.make_async_copy(ratings.at[slot], stack.at[place], rating_sems.at[place])
            copy.start() if start else copy.wait()

        @pl.when(slot >= 128)
        def _():
            copy = pltpu.make_async_copy(mate_ratings.at[slot - 128], stack.at[place], rating_sems.at[place])
            copy.start() if start else copy.wait()

    ahead = SLOTS - GROUP

    def begin(n, carry):
        fetch(n, True)
        return carry

    lax.fori_loop(0, jnp.minimum(groups * GROUP, ahead), begin, 0)

    def clear(k, carry):
        user_sum[k] = jnp.zeros((edge, 128), jnp.float32)
        return carry

    lax.fori_loop(0, 128, clear, 0)
    item_sum[...] = jnp.zeros_like(item_sum)
    load.wait()

    def step(g, carry):
        first = g * GROUP
        for k in range(GROUP):
            fetch(first + k, False)
        records = []
        for k in range(GROUP):
            n = first + k
            entry = order[n]
            item = lax.rem(entry, 8)
            block = lax.rem(entry // 8, 256)
            tile = (block // 16) * 8 + lax.rem(block, 8)
            user_tile = users[tile]
            item_tile = items[item]
            predicted = lax.dot_general(
                user_tile, item_tile, (((1,), (1,)), ((), ())), preferred_element_type=jnp.float32
            )
            scores = stack[lax.rem(n, SLOTS)]
            floor = jnp.where(n < count, 0, 1 << 20)
            errors = jnp.where(
                scores > floor, predicted - (scores.astype(jnp.float32) - 3.0), 0.0
            ).astype(jnp.bfloat16)
            records.append((tile, item, user_tile, item_tile, errors))
        terms = []
        for tile, item, user_tile, item_tile, errors in records:
            user_term = jnp.dot(errors, item_tile, preferred_element_type=jnp.float32)
            item_term = lax.dot_general(
                errors, user_tile, (((0,), (0,)), ((), ())), preferred_element_type=jnp.float32
            )
            terms.append((tile, item, user_term, item_term))
        for tile, item, user_term, item_term in terms:
            user_sum[tile] += user_term
            item_sum[item] += item_term
        for k in range(GROUP):
            later = first + k + ahead

            @pl.when(later < groups * GROUP)
            def _(later=later):
                fetch(later, True)

        return carry

    lax.fori_loop(0, groups, step, 0)
    outs = [
        pltpu.make_async_copy(user_sum, user_out, out_sems.at[0]),
        pltpu.make_async_copy(item_sum, item_out, out_sems.at[1]),
    ]
    for copy in outs:
        copy.start()
    for copy in outs:
        copy.wait()


def local(core, lists, mate_lists, users, items, ratings, mate_ratings):
    smem = pl.BlockSpec(memory_space=pltpu.SMEM)
    hbm = pl.BlockSpec(memory_space=pltpu.HBM)
    return pl.pallas_call(
        local_kernel,
        out_shape=(
            jax.ShapeDtypeStruct((128, 128, 128), jnp.float32),
            jax.ShapeDtypeStruct((8, 128, 128), jnp.float32),
        ),
        in_specs=[smem, smem, smem, hbm, pl.BlockSpec(memory_space=pltpu.VMEM), hbm, hbm],
        out_specs=(hbm, hbm),
        scratch_shapes=[
            pltpu.VMEM((128, 128, 128), jnp.bfloat16),
            pltpu.VMEM((128, 128, 128), jnp.float32),
            pltpu.VMEM((8, 128, 128), jnp.float32),
            pltpu.VMEM((SLOTS, 128, 128), jnp.int32),
            pltpu.SMEM((256 + GROUP,), jnp.int32),
            pltpu.SemaphoreType.DMA,
            pltpu.SemaphoreType.DMA((SLOTS,)),
            pltpu.SemaphoreType.DMA((2,)),
        ],
        compiler_params=pltpu.CompilerParams(vmem_limit_bytes=40 * 2**20),
    )(core, lists, mate_lists, users, items, ratings, mate_ratings)


user_step = 0.1
item_step = 0.04
shrinkage = 0.1
SCALE_ROWS = 16


def encode(value, buffer):
    rows = value.shape[0]
    folded = value.reshape(rows // 8, 8, 128)
    peak = jnp.maximum(jnp.max(jnp.abs(folded), axis=0), 1e-30)
    power = jnp.ceil(jnp.log2(peak))
    whole = jnp.round(folded * jnp.exp2(14.0 - power)).reshape(rows, 128)
    buffer[0:rows] = whole.astype(jnp.int32).astype(jnp.int16)
    both = jnp.concatenate([power, power], axis=0)
    buffer[rows:rows + SCALE_ROWS] = both.astype(jnp.int32).astype(jnp.int16)


def decode(buffer):
    rows = buffer.shape[0] - SCALE_ROWS
    power = buffer[rows:rows + SCALE_ROWS].astype(jnp.float32)[0:8]
    folded = buffer[0:rows].astype(jnp.float32).reshape(rows // 8, 8, 128)
    return (folded * jnp.exp2(power - 14.0)).reshape(rows, 128)


def reduce_kernel(
    sums_hbm, item_sums, own_users, own_items, new_users, new_items,
    sums, plane_out, plane_in, column_out, column_in, total, last_out, last_in, grads,
    item_in, item_half, item_out, item_z, item_pair_out, item_pair_in, item_grads,
    load_sems, plane_send, plane_recv, column_send, column_recv, last_send, last_recv,
    grad_send, grad_recv, item_send, item_recv, item_z_send, item_z_recv, item_back_send, item_back_recv,
):
    z, ylo, yhi, x, c = here()
    y = yhi * 2 + ylo
    q = yhi * 4 + x

    def turn(v, k, n):
        return lax.rem(v + k, n)

    def copy(src, dst, send_sem, recv_sem, where):
        return pltpu.make_async_remote_copy(
            src_ref=src, dst_ref=dst, send_sem=send_sem, recv_sem=recv_sem,
            device_id=where, device_id_type=MESH,
        )

    def offset_of(i):
        return 4 + (1 - 2 * lax.rem(i, 2)) * ((i + 1) // 2)

    def load_of(i):
        zz = turn(z, offset_of(i), 8)
        return pltpu.make_async_copy(sums_hbm.at[zz], sums.at[zz], load_sems.at[i])

    for i in range(8):
        load_of(i).start()

    barrier = pltpu.get_barrier_semaphore()
    others = [device(z, y, turn(x, k, 4), c) for k in (1, 2, 3)]
    others += [device(z, turn(y, k, 4), x, c) for k in (1, 2, 3)]
    others += [device(z, turn(y, 2, 4), turn(x, k, 4), c) for k in (1, 2, 3)]
    others += [device(turn(z, k, 8), y, x, c) for k in range(1, 8)]
    others += [device(z, y, x, 1 - c)]
    for other in others:
        pl.semaphore_signal(barrier, inc=1, device_id=other, device_id_type=MESH)
    pl.semaphore_wait(barrier, len(others))

    mate = device(z, y, x, 1 - c)
    pair = device(z, yhi * 2 + 1 - ylo, x, c)
    item_first = copy(item_sums.at[pl.ds((1 - c) * 4, 4)], item_in, item_send.at[0], item_recv.at[0], mate)
    item_first.start()

    def plane_where(part, k):
        return device(z, y, turn(x, k, 4), c) if part == 0 else device(z, turn(y, k, 4), x, c)

    def plane_block(part, zz, k):
        if part == 0:
            return sums[zz, :, :, turn(x, k, 4), 0:64].reshape(256, 128)
        other = turn(y, k, 4)
        return sums[zz, lax.rem(other, 2), other // 2, :, 64:128].reshape(256, 128)

    def plane_copy(part, i, k):
        return copy(
            plane_out.at[part, i, k - 1], plane_in.at[part, i, k - 1],
            plane_send.at[part, i, k - 1], plane_recv.at[part, i, k - 1], plane_where(part, k),
        )

    def plane_step(i, carry):
        zz = turn(z, offset_of(i), 8)
        load_of(i).wait()
        for k in (2, 1, 3):
            for part in (0, 1):
                encode(plane_block(part, zz, k), plane_out.at[part, i, k - 1])
                plane_copy(part, i, k).start()
        return carry

    def item_z_copy(o):
        return copy(
            item_out.at[o - 1], item_z.at[o - 1], item_z_send.at[o - 1], item_z_recv.at[o - 1],
            device(turn(z, o, 8), y, x, c),
        )

    lax.fori_loop(0, 1, plane_step, 0)
    item_first.wait_recv()
    item_half[...] = item_sums[pl.ds(c * 4, 4)].reshape(512, 128) + item_in[...].reshape(512, 128)

    def item_step_z(o, carry):
        zz = turn(z, o, 8)
        encode(item_half[pl.ds(pl.multiple_of(zz * 64, 64), 64)], item_out.at[o - 1])
        item_z_copy(o).start()
        return carry

    lax.fori_loop(1, 8, item_step_z, 0)
    lax.fori_loop(1, 8, plane_step, 0)

    def column_copy(part, i):
        return copy(
            column_out.at[part, i], column_in.at[part, i],
            column_send.at[part, i], column_recv.at[part, i],
            device(turn(z, offset_of(i), 8), y, x, c),
        )

    def plane_total(part, i):
        value = plane_block(part, turn(z, offset_of(i), 8), 0)
        for k in (1, 2, 3):
            plane_copy(part, i, k).wait_recv()
        for k in (1, 2, 3):
            value += decode(plane_in.at[part, i, k - 1])
        return value

    def column_step(i, carry):
        for part in (0, 1):
            encode(plane_total(part, i), column_out.at[part, i])
            column_copy(part, i).start()
        return carry

    lax.fori_loop(0, 1, column_step, 0)
    def item_gather(o, value):
        item_z_copy(o).wait_recv()
        return value + decode(item_z.at[o - 1])

    item_total = lax.fori_loop(
        1, 8, item_gather, item_half[pl.ds(pl.multiple_of(z * 64, 64), 64)]
    )
    item_pair_out[...] = item_total
    item_pair = copy(
        item_pair_out.at[pl.ds(pl.multiple_of((1 - ylo) * 32, 32), 32)], item_pair_in,
        item_send.at[1], item_recv.at[1], pair,
    )
    item_pair.start()
    lax.fori_loop(1, 3, column_step, 0)
    item_pair.wait_recv()
    encode(
        item_pair_out[pl.ds(pl.multiple_of(ylo * 32, 32), 32)] + item_pair_in[...],
        item_grads.at[c, z, ylo],
    )
    item_share = copy(
        item_grads.at[c, z, ylo], item_grads.at[c, z, ylo], item_send.at[2], item_recv.at[2], pair
    )
    item_share.start()
    lax.fori_loop(3, 4, column_step, 0)
    item_share.wait_recv()

    def item_back(o):
        return copy(
            item_grads.at[c, z], item_grads.at[c, z], item_back_send.at[o - 1], item_back_recv.at[o - 1],
            device(turn(z, o, 8), y, x, c),
        )

    def item_back_start(o, carry):
        item_back(o).start()
        return carry

    lax.fori_loop(1, 8, item_back_start, 0)
    lax.fori_loop(4, 7, column_step, 0)
    for part in (0, 1):
        total[part] = plane_total(part, 7)

    def item_back_wait(o, carry):
        item_back(o).wait_recv()
        return carry

    lax.fori_loop(1, 8, item_back_wait, 0)
    item_last = copy(item_grads.at[c], item_grads.at[c], item_send.at[3], item_recv.at[3], mate)
    item_last.start()

    def column_gather(i, carry):
        for part in (0, 1):
            column_copy(part, i).wait_recv()
            total[part] += decode(column_in.at[part, i])
        return carry

    lax.fori_loop(0, 7, column_gather, 0)

    def last_rows(part, k):
        if part == 0:
            other = turn(y, k, 4)
            place = lax.rem(other, 2) * 2 + other // 2
        else:
            place = turn(x, k, 4)
        return total[part, pl.ds(pl.multiple_of(place * 64, 64), 64)]

    def last_copy(part, k):
        return copy(
            last_out.at[part, k - 1], last_in.at[part, k - 1],
            last_send.at[part, k - 1], last_recv.at[part, k - 1], plane_where(1 - part, k),
        )

    for k in (2, 1, 3):
        for part in (0, 1):
            encode(last_rows(part, k), last_out.at[part, k - 1])
            last_copy(part, k).start()

    item_last.wait_recv()

    def item_finish(n, carry):
        grad = decode(item_grads.at[n // 16, lax.rem(n // 2, 8), lax.rem(n, 2)])
        rows = pl.ds(pl.multiple_of(n * 32, 32), 32)
        now = own_items[rows].astype(jnp.float32)
        new_items[rows] = now - item_step * (grad + shrinkage * now)
        return carry

    lax.fori_loop(0, 32, item_finish, 0)

    halves = []
    for part in (0, 1):
        value = last_rows(part, 0)
        for k in (1, 2, 3):
            last_copy(part, k).wait_recv()
            value += decode(last_in.at[part, k - 1])
        halves.append(value)
    encode(jnp.concatenate(halves, axis=0), grads.at[q])

    def grad_copy(m):
        other = turn(q, m, 8)
        return copy(
            grads.at[q], grads.at[q], grad_send.at[m - 1], grad_recv.at[m - 1],
            device(z, (other // 4) * 2 + ylo, lax.rem(other, 4), c),
        )

    for m in range(1, 8):
        grad_copy(m).start()

    def plane_drain(i, carry):
        for part in (0, 1):
            for k in (1, 2, 3):
                plane_copy(part, i, k).wait_send()
        return carry

    def column_drain(i, carry):
        for part in (0, 1):
            column_copy(part, i).wait_send()
        item_z_copy(i + 1).wait_send()
        item_back(i + 1).wait_send()
        return carry

    lax.fori_loop(0, 8, plane_drain, 0)
    lax.fori_loop(0, 7, column_drain, 0)
    for part in (0, 1):
        for k in (1, 2, 3):
            last_copy(part, k).wait_send()
    for early in (item_first, item_pair, item_share, item_last):
        early.wait_send()

    for m in range(1, 8):
        grad_copy(m).wait_recv()

    def user_finish(j, carry):
        grad = decode(grads.at[j])
        rows = pl.ds(pl.multiple_of(j * 128, 128), 128)
        now = own_users[rows].astype(jnp.float32)
        new_users[rows] = now - user_step * (grad + shrinkage * now)
        return carry

    lax.fori_loop(0, 8, user_finish, 0)
    for m in range(1, 8):
        grad_copy(m).wait_send()


def reduce(sums, item_sums, own_users, own_items):
    vmem = pl.BlockSpec(memory_space=pltpu.VMEM)
    dma = pltpu.SemaphoreType.DMA
    i16, f32 = jnp.int16, jnp.float32
    plane = (2, 8, 3, 256 + SCALE_ROWS, 128)
    column = (2, 7, 256 + SCALE_ROWS, 128)
    last = (2, 3, 64 + SCALE_ROWS, 128)
    return pl.pallas_call(
        reduce_kernel,
        out_shape=(
            jax.ShapeDtypeStruct((1024, 128), f32),
            jax.ShapeDtypeStruct((1024, 128), f32),
        ),
        in_specs=[pl.BlockSpec(memory_space=pltpu.HBM), vmem, vmem, vmem],
        out_specs=(vmem, vmem),
        scratch_shapes=[
            pltpu.VMEM((8, 2, 2, 4, 128, 128), f32),
            pltpu.VMEM(plane, i16), pltpu.VMEM(plane, i16),
            pltpu.VMEM(column, i16), pltpu.VMEM(column, i16),
            pltpu.VMEM((2, 256, 128), f32),
            pltpu.VMEM(last, i16), pltpu.VMEM(last, i16),
            pltpu.VMEM((8, 128 + SCALE_ROWS, 128), i16),
            pltpu.VMEM((4, 128, 128), f32), pltpu.VMEM((512, 128), f32),
            pltpu.VMEM((7, 64 + SCALE_ROWS, 128), i16), pltpu.VMEM((7, 64 + SCALE_ROWS, 128), i16),
            pltpu.VMEM((64, 128), f32), pltpu.VMEM((32, 128), f32),
            pltpu.VMEM((2, 8, 2, 32 + SCALE_ROWS, 128), i16),
            dma((8,)), dma((2, 8, 3)), dma((2, 8, 3)), dma((2, 7)), dma((2, 7)),
            dma((2, 3)), dma((2, 3)), dma((7,)), dma((7,)),
            dma((4,)), dma((4,)), dma((7,)), dma((7,)), dma((7,)), dma((7,)),
        ],
        compiler_params=pltpu.CompilerParams(
            collective_id=1, has_side_effects=True, vmem_limit_bytes=40 * 2**20
        ),
    )(sums.reshape(8, 2, 2, 4, 128, 128), item_sums, own_users, own_items)


def body(user_factors, item_factors, block_user, block_item, live_blocks, ratings):
    slots = ratings.shape[2]
    scores = ratings.reshape(slots, 128, 128)
    lists = jnp.concatenate(
        [
            block_user.reshape(1, slots),
            block_item.reshape(1, slots),
            jnp.broadcast_to(live_blocks.reshape(1, 1), (1, slots)),
            jnp.zeros((5, slots), jnp.int32),
        ],
        axis=0,
    )
    users, mate_scores, mate_lists = gather(user_factors, scores, lists)
    core = lax.rem(lax.axis_index("user"), 2).astype(jnp.int32).reshape(1)
    user_sums, item_sums = local(
        core, lists, mate_lists, users.reshape(128, 128, 128), item_factors.reshape(8, 128, 128),
        scores, mate_scores,
    )
    return reduce(user_sums, item_sums, user_factors, item_factors)


def solution(mesh):
    return jax.shard_map(
        body,
        mesh=mesh,
        in_specs=(
            P("user", None),
            P("item", None),
            P("user", "item", None),
            P("user", "item", None),
            P("user", "item"),
            P("user", "item", None, None, None),
        ),
        out_specs=(P("user", None), P("item", None)),
        check_vma=False,
    )
```

time: 662 us -> 121 us (0.18)
  waiting for transfers between devices: 565 us -> 0 us
  Pallas kernels: 0 us -> 108 us
  matrix products: 44.1 us -> 0 us
  local copies, waits for them, and re-layouts: 31.4 us -> 10.1 us
  between operations: 14.5 us -> 1.38 us
    psum x2 -> x0, waiting for transfers between devices: 319 us -> none  [the longest x1 230 us: body(): item_grad = lax.psum(item_local.reshape(-1, factor_dim), 'user')]
    reduce_scatter x1 -> x0, waiting for transfers between devices: 173 us -> none  [body(): lax.psum_scatter(summed.reshape(local_rows * lax.axis_size('user'), facto...]
    pallas_call x0 -> x3, Pallas kernels: none -> 108 us  [the longest x1 64.1 us: reduce(): pl.pallas_call(reduce_kernel, out_shape=(jax.ShapeDtypeStruct((1024, 128)...]
    all_gather x1 -> x0, waiting for transfers between devices: 71.8 us -> none  [body(): everyone = lax.all_gather(user_factors, 'user', axis=0, tiled=True)]
    dot_general x5 -> x0, matrix products: 44.1 us -> none  [the longest x1 15.5 us: body(): jnp.einsum('bs,bir->sir', selector, user_terms, precision=lax.Precision.H...]
    dot_general x2 -> x0, local copies, waits for them, and re-layouts: 20.9 us -> none  [the longest x1 20 us: body(): jnp.einsum('bs,bir->sir', selector, user_terms, precision=lax.Precision.H...]
    gather x2 -> x0, local copies, waits for them, and re-layouts: 10.4 us -> none  [the longest x1 6.4 us: body(): user_tiles = everyone.reshape(-1, tile_edge, factor_dim)[user_block]]
    unnamed x12 -> x14, local copies, waits for them, and re-layouts: 0.03 us -> 9.92 us
  transfers between devices with their start and end apart: 4 -> 0, of which waited for: 4 -> 0; matrix products, arithmetic and copies ran while one was open for 3% -> 0% of each run, Pallas kernels for 0% -> 0%
where the time goes in v1:
time: 121 us; the launch traced here: 120 us
  Pallas kernels  108 us (89%)
  local copies, waits for them, and re-layouts  10.1 us (8%)
  between operations  1.38 us (1%)
    pallas_call x1, Pallas kernels, reduce(): pl.pallas_call(reduce_kernel, out_shape=(jax.ShapeDtypeStruct((1024, 128)...  64.1 us
    pallas_call x1, Pallas kernels, gather(): pl.pallas_call(functools.partial(gather_kernel, (ROWS_A, ROWS_B, ROWS_C))...  36.7 us
    unnamed x14, local copies, waits for them, and re-layouts  9.92 us
    pallas_call x1, Pallas kernels, local(): pl.pallas_call(local_kernel, out_shape=(jax.ShapeDtypeStruct((128, 128, 1...  7.08 us

profile of v1, /device:TPU:6, one launch (start us, length us, event | category | flops | bytes accessed | tf_op | source)
XLA Modules:
  0.0 120.1 jit_solution(15911714621129809015)
XLA Ops:
  0.6 0.0 copy-start.3
  1.3 0.1 pad.2.clone
  1.4 0.1 pad.3.clone
  1.5 0.7 add_add_fusion.lists
  2.2 0.0 copy-start.4
  2.2 0.9 copy-done.4
  3.2 36.7 %shard_map.77 = (bf16[8,2,2,4,128,128]{5,4,3,2,1,0:T(8,128)(2,1)S(1)}, s32[128,128,128]{2,1,0:T(8,128)S(1)}, s32[8,128]{1,0:T(8,128)S(1)}) custom-call(bf16[2,4,128,128]{3,2,1,0:T(8,128)(2,1)S(1)} %bitcast.15, s32[128,128,128]{2,1,0:T(8,128)} %bitcast.16, s32[8,128]{1,0:T(8,128)S(1)} %add_add_fusion.lists), custom_call_target="tpu_custom_call" | custom-call | tf_op jit(solution)/shard_map/pallas_call | solution.py:208
  39.9 0.0 copy-start
  39.9 3.2 %copy-done = s32[128,128,128]{2,1,0:T(8,128)} copy-done((s32[128,128,128]{2,1,0:T(8,128)}, s32[128,128,128]{2,1,0:T(8,128)S(1)}, u32[]{:S(2)}) %copy-start) | copy-done | bytes 8388632
  43.1 0.0 copy-start.1
  43.1 2.0 %copy-done.1 = bf16[8,2,2,4,128,128]{5,4,3,2,1,0:T(8,128)(2,1)} copy-done((bf16[8,2,2,4,128,128]{5,4,3,2,1,0:T(8,128)(2,1)}, bf16[8,2,2,4,128,128]{5,4,3,2,1,0:T(8,128)(2,1)S(1)}, u32[]{:S(2)}) %copy-start.1) | copy-done | bytes 4194328
  45.1 0.0 copy-done.3
  45.1 0.0 copy-start.2
  45.1 2.2 %copy-done.2 = bf16[8,2,2,4,128,128]{5,4,3,2,1,0:T(8,128)(2,1)S(1)} copy-done((bf16[8,2,2,4,128,128]{5,4,3,2,1,0:T(8,128)(2,1)S(1)}, bf16[8,2,2,4,128,128]{5,4,3,2,1,0:T(8,128)(2,1)}, u32[]{:S(2)}) %copy-start.2) | copy-done | bytes 4194328
  47.3 0.0 copy-start.5
  47.3 7.1 %shard_map.78 = (f32[128,128,128]{2,1,0:T(8,128)S(1)}, f32[8,128,128]{2,1,0:T(8,128)S(1)}) custom-call(s32[1]{0:T(128)} %bitcast.core, s32[8,128]{1,0:T(8,128)S(1)} %add_add_fusion.lists, s32[8,128]{1,0:T(8,128)S(1)} %get-tuple-element.7.mate_lists, bf16[128,128,128]{2,1,0:T(8,128)(2,1)S(1)} %bitcast.13, bf16[8,128,128]{2,1,0:T(8,128)(2,1)S(1)} %bitcast.14, ...), custom_call_target="tpu_custom_call" | custom-call | tf_op jit(solution)/shard_map/pallas_call | solution.py:346
  54.4 0.0 copy-done.5
  54.4 64.1 %shard_map.79 = (f32[1024,128]{1,0:T(8,128)S(1)}, f32[1024,128]{1,0:T(8,128)S(1)}) custom-call(f32[8,2,2,4,128,128]{5,4,3,2,1,0:T(8,128)S(1)} %bitcast.12, f32[8,128,128]{2,1,0:T(8,128)S(1)} %get-tuple-element.11.item_sums, bf16[1024,128]{1,0:T(8,128)(2,1)S(1)} %copy-done.5, bf16[1024,128]{1,0:T(8,128)(2,1)S(1)} %copy-done.3), custom_call_target="tpu_custom_call" | custom-call | tf_op jit(solution)/shard_map/pallas_call | solution.py:651
  118.5 0.8 copy.11
  119.3 0.8 copy.12
  (1 shorter events, 0.0 us)
Async XLA Ops:
  0.6 44.5 %copy-start.3 = (bf16[1024,128]{1,0:T(8,128)(2,1)S(1)}, bf16[1024,128]{1,0:T(8,128)(2,1)}, u32[]{:S(2)}) copy-start(bf16[1024,128]{1,0:T(8,128)(2,1)} %own_items.1) | copy-start | bytes 786436
  2.2 0.9 copy-start.4
  39.9 3.2 %copy-start = (s32[128,128,128]{2,1,0:T(8,128)}, s32[128,128,128]{2,1,0:T(8,128)S(1)}, u32[]{:S(2)}) copy-start(s32[128,128,128]{2,1,0:T(8,128)S(1)} %get-tuple-element.9.mate_ratings) | copy-start | bytes 25165828
  43.1 2.0 %copy-start.1 = (bf16[8,2,2,4,128,128]{5,4,3,2,1,0:T(8,128)(2,1)}, bf16[8,2,2,4,128,128]{5,4,3,2,1,0:T(8,128)(2,1)S(1)}, u32[]{:S(2)}) copy-start(bf16[8,2,2,4,128,128]{5,4,3,2,1,0:T(8,128)(2,1)S(1)} %get-tuple-element.8) | copy-start | bytes 12582916
  45.1 2.2 %copy-start.2 = (bf16[8,2,2,4,128,128]{5,4,3,2,1,0:T(8,128)(2,1)S(1)}, bf16[8,2,2,4,128,128]{5,4,3,2,1,0:T(8,128)(2,1)}, u32[]{:S(2)}) copy-start(bf16[8,2,2,4,128,128]{5,4,3,2,1,0:T(8,128)(2,1)} %copy-done.1) | copy-start | bytes 12582916
  47.3 7.1 %copy-start.5 = (bf16[1024,128]{1,0:T(8,128)(2,1)S(1)}, bf16[1024,128]{1,0:T(8,128)(2,1)}, u32[]{:S(2)}) copy-start(bf16[1024,128]{1,0:T(8,128)(2,1)} %own_users.1) | copy-start | bytes 786436

commit v2 on v1

--- a/solution.py
+++ b/solution.py
@@ -69,12 +69,16 @@
 GATHER_COPIES = 160
 
 
-def gather_kernel(split, own, ratings, lists, users, mate_ratings, mate_lists, local_sem, send_sems, recv_sems):
+def gather_kernel(split, own, ratings, lists, users, all_ratings, all_lists, local_sems, send_sems, recv_sems):
     z, ylo, yhi, x, c = here()
     y = yhi * 2 + ylo
     near = neighbours()
-    keep = pltpu.make_async_copy(own, users.at[z, ylo], local_sem)
+    keep = pltpu.make_async_copy(own, users.at[z, ylo], local_sems.at[0])
     keep.start()
+    near_lists = pltpu.make_async_copy(lists, all_lists.at[c], local_sems.at[1])
+    near_lists.start()
+    near_ratings = pltpu.make_async_copy(ratings, all_ratings.at[c], local_sems.at[2])
+    near_ratings.start()
     meet(near)
     send = Sender(send_sems, recv_sems)
     keep.wait()
@@ -154,8 +158,8 @@
     x_send(0, 0)
     y_send(0)
     z_send("C", 1)
-    far = send(ratings, mate_ratings, near["mate"])
-    far_lists = send(lists, mate_lists, near["mate"])
+    far = send(ratings, all_ratings.at[c], near["mate"])
+    far_lists = send(lists, all_lists.at[c], near["mate"])
     before = [0]
     for step in (1, 2, 3, 4):
         offsets = [-step, step] if step < 4 else [4]
@@ -198,100 +202,76 @@
     z_wait("D", 4)
     for copy in last:
         copy.wait_recv()
+    near_lists.wait()
+    near_ratings.wait()
     far.wait_recv()
     far_lists.wait_recv()
     send.drain()
 
 
 def gather(user_factors, ratings, lists, vmem=True):
-    space = pltpu.VMEM if vmem else pltpu.HBM
+    space = pltpu.VMEM if vmem else pl.ANY
     return pl.pallas_call(
         functools.partial(gather_kernel, (ROWS_A, ROWS_B, ROWS_C)),
         out_shape=(
             jax.ShapeDtypeStruct((8, 2, 2, 4, 128, 128), jnp.bfloat16),
-            jax.ShapeDtypeStruct(ratings.shape, jnp.int32),
-            jax.ShapeDtypeStruct(lists.shape, jnp.int32),
+            jax.ShapeDtypeStruct((2, *ratings.shape), jnp.int32),
+            jax.ShapeDtypeStruct((2, *lists.shape), jnp.int32),
         ),
         in_specs=[
-            pl.BlockSpec(memory_space=space),
+            pl.BlockSpec(memory_space=pltpu.HBM),
             pl.BlockSpec(memory_space=pltpu.HBM),
             pl.BlockSpec(memory_space=pltpu.VMEM),
         ],
         out_specs=(
             pl.BlockSpec(memory_space=space),
-            pl.BlockSpec(memory_space=pltpu.HBM),
+            pl.BlockSpec(memory_space=space),
             pl.BlockSpec(memory_space=pltpu.VMEM),
         ),
         scratch_shapes=[
-            pltpu.SemaphoreType.DMA,
+            pltpu.SemaphoreType.DMA((3,)),
             pltpu.SemaphoreType.DMA((GATHER_COPIES,)),
             pltpu.SemaphoreType.DMA((GATHER_COPIES,)),
         ],
         compiler_params=pltpu.CompilerParams(
-            collective_id=0, has_side_effects=True, vmem_limit_bytes=40 * 2**20
+            collective_id=0, has_side_effects=True, vmem_limit_bytes=8 * 2**20
         ),
-    )(user_factors.reshape(2, 4, 128, 128), ratings, lists)
-
-
-GROUP = 4
-SLOTS = 32
-
-
-def local_kernel(core, lists, mate_lists, users_hbm, items, ratings, mate_ratings, user_out, item_out, users, user_sum, item_sum, stack, order, users_sem, rating_sems, out_sems):
-    load = pltpu.make_async_copy(users_hbm, users, users_sem)
-    load.start()
+    )(
+        pltpu.with_memory_space_constraint(user_factors.reshape(2, 4, 128, 128), pltpu.HBM),
+        pltpu.with_memory_space_constraint(ratings, pltpu.HBM),
+        lists,
+    )
+
+
+GROUP = 16
+
+
+def local_kernel(core, lists, users, items, ratings, user_sum, item_sum, order):
     mine = core[0]
     edge = ratings.shape[1]
 
-    def scan(table, base):
+    def scan(table):
         def visit(slot, count):
-            block = table[0, slot]
-            item = table[1, slot]
-            order[count] = (((base + slot) * 256 + block) * 8) + item
+            block = lists[table, 0, slot]
+            order[count] = ((table * 128 + slot) * 256 + block) * 8 + lists[table, 1, slot]
             keep = lax.rem(block // 8, 2) == mine
             return count + keep.astype(jnp.int32)
         return visit
 
-    count = lax.fori_loop(0, lists[2, 0], scan(lists, 0), jnp.int32(0))
-    count = lax.fori_loop(0, mate_lists[2, 0], scan(mate_lists, 128), count)
-    groups = (count + GROUP - 1) // GROUP
+    count = lax.fori_loop(0, lists[0, 2, 0], scan(0), jnp.int32(0))
+    count = lax.fori_loop(0, lists[1, 2, 0], scan(1), count)
     for k in range(GROUP):
         order[count + k] = 0
 
-    def fetch(n, start):
-        slot = order[n] // 2048
-        place = lax.rem(n, SLOTS)
-
-        @pl.when(slot < 128)
-        def _():
-            copy = pltpu.make_async_copy(ratings.at[slot], stack.at[place], rating_sems.at[place])
-            copy.start() if start else copy.wait()
-
-        @pl.when(slot >= 128)
-        def _():
-            copy = pltpu.make_async_copy(mate_ratings.at[slot - 128], stack.at[place], rating_sems.at[place])
-            copy.start() if start else copy.wait()
-
-    ahead = SLOTS - GROUP
-
-    def begin(n, carry):
-        fetch(n, True)
-        return carry
-
-    lax.fori_loop(0, jnp.minimum(groups * GROUP, ahead), begin, 0)
-
     def clear(k, carry):
         user_sum[k] = jnp.zeros((edge, 128), jnp.float32)
         return carry
 
     lax.fori_loop(0, 128, clear, 0)
     item_sum[...] = jnp.zeros_like(item_sum)
-    load.wait()
 
     def step(g, carry):
         first = g * GROUP
-        for k in range(GROUP):
-            fetch(first + k, False)
         records = []
         for k in range(GROUP):
             n = first + k
@@ -304,7 +284,7 @@
             predicted = lax.dot_general(
                 user_tile, item_tile, (((1,), (1,)), ((), ())), preferred_element_type=jnp.float32
             )
-            scores = stack[lax.rem(n, SLOTS)]
+            scores = ratings[entry // 2048]
             floor = jnp.where(n < count, 0, 1 << 20)
             errors = jnp.where(
                 scores > floor, predicted - (scores.astype(jnp.float32) - 3.0), 0.0
@@ -320,49 +300,25 @@
         for tile, item, user_term, item_term in terms:
             user_sum[tile] += user_term
             item_sum[item] += item_term
-        for k in range(GROUP):
-            later = first + k + ahead
-
-            @pl.when(later < groups * GROUP)
-            def _(later=later):
-                fetch(later, True)
-
-        return carry
-
-    lax.fori_loop(0, groups, step, 0)
-    outs = [
-        pltpu.make_async_copy(user_sum, user_out, out_sems.at[0]),
-        pltpu.make_async_copy(item_sum, item_out, out_sems.at[1]),
-    ]
-    for copy in outs:
-        copy.start()
-    for copy in outs:
-        copy.wait()
-
-
-def local(core, lists, mate_lists, users, items, ratings, mate_ratings):
+        return carry
+
+    lax.fori_loop(0, (count + GROUP - 1) // GROUP, step, 0)
+
+
+def local(core, lists, users, items, ratings):
     smem = pl.BlockSpec(memory_space=pltpu.SMEM)
-    hbm = pl.BlockSpec(memory_space=pltpu.HBM)
+    vmem = pl.BlockSpec(memory_space=pltpu.VMEM)
     return pl.pallas_call(
         local_kernel,
         out_shape=(
             jax.ShapeDtypeStruct((128, 128, 128), jnp.float32),
             jax.ShapeDtypeStruct((8, 128, 128), jnp.float32),
         ),
-        in_specs=[smem, smem, smem, hbm, pl.BlockSpec(memory_space=pltpu.VMEM), hbm, hbm],
-        out_specs=(hbm, hbm),
-        scratch_shapes=[
-            pltpu.VMEM((128, 128, 128), jnp.bfloat16),
-            pltpu.VMEM((128, 128, 128), jnp.float32),
-            pltpu.VMEM((8, 128, 128), jnp.float32),
-            pltpu.VMEM((SLOTS, 128, 128), jnp.int32),
-            pltpu.SMEM((256 + GROUP,), jnp.int32),
-            pltpu.SemaphoreType.DMA,
-            pltpu.SemaphoreType.DMA((SLOTS,)),
-            pltpu.SemaphoreType.DMA((2,)),
-        ],
-        compiler_params=pltpu.CompilerParams(vmem_limit_bytes=40 * 2**20),
-    )(core, lists, mate_lists, users, items, ratings, mate_ratings)
+        in_specs=[smem, smem, vmem, vmem, vmem],
+        out_specs=(vmem, vmem),
+        scratch_shapes=[pltpu.SMEM((256 + GROUP,), jnp.int32)],
+        compiler_params=pltpu.CompilerParams(vmem_limit_bytes=8 * 2**20),
+    )(core, lists, users, items, ratings)
 
 
 user_step = 0.1
@@ -390,10 +346,10 @@
 
 
 def reduce_kernel(
-    sums_hbm, item_sums, own_users, own_items, new_users, new_items,
-    sums, plane_out, plane_in, column_out, column_in, total, last_out, last_in, grads,
+    sums, item_sums, own_users, own_items, new_users, new_items,
+    half_out, half_in, near_out, near_in, far_out, far_in, column_out, column_in, total, last_out, last_in, grads,
     item_in, item_half, item_out, item_z, item_pair_out, item_pair_in, item_grads,
-    load_sems, plane_send, plane_recv, column_send, column_recv, last_send, last_recv,
+    half_send, half_recv, near_send, near_recv, far_send, far_recv, column_send, column_recv, last_send, last_recv,
     grad_send, grad_recv, item_send, item_recv, item_z_send, item_z_recv, item_back_send, item_back_recv,
 ):
     z, ylo, yhi, x, c = here()
@@ -411,13 +367,6 @@
 
     def offset_of(i):
         return 4 + (1 - 2 * lax.rem(i, 2)) * ((i + 1) // 2)
-
-    def load_of(i):
-        zz = turn(z, offset_of(i), 8)
-        return pltpu.make_async_copy(sums_hbm.at[zz], sums.at[zz], load_sems.at[i])
-
-    for i in range(8):
-        load_of(i).start()
 
     barrier = pltpu.get_barrier_semaphore()
     others = [device(z, y, turn(x, k, 4), c) for k in (1, 2, 3)]
@@ -443,19 +392,44 @@
         other = turn(y, k, 4)
         return sums[zz, lax.rem(other, 2), other // 2, :, 64:128].reshape(256, 128)
 
-    def plane_copy(part, i, k):
+    def toward(part, way):
+        return plane_where(part, 1 if way == 0 else 3)
+
+    def half_copy(part, i, way):
         return copy(
-            plane_out.at[part, i, k - 1], plane_in.at[part, i, k - 1],
-            plane_send.at[part, i, k - 1], plane_recv.at[part, i, k - 1], plane_where(part, k),
-        )
-
-    def plane_step(i, carry):
+            half_out.at[part, i, way], half_in.at[part, i, way],
+            half_send.at[part, i, way], half_recv.at[part, i, way], toward(part, way),
+        )
+
+    def near_copy(part, i, way):
+        return copy(
+            near_out.at[part, i, way], near_in.at[part, i, way],
+            near_send.at[part, i, way], near_recv.at[part, i, way], toward(part, way),
+        )
+
+    def add_half(value, way, extra):
+        if way == 0:
+            return jnp.concatenate([value[0:128] + extra, value[128:256]], axis=0)
+        return jnp.concatenate([value[0:128], value[128:256] + extra], axis=0)
+
+    def half_step(i, carry):
         zz = turn(z, offset_of(i), 8)
-        load_of(i).wait()
-        for k in (2, 1, 3):
+        for way in (0, 1):
             for part in (0, 1):
-                encode(plane_block(part, zz, k), plane_out.at[part, i, k - 1])
-                plane_copy(part, i, k).start()
+                block = plane_block(part, zz, 2)[128 * way:128 * way + 128]
+                encode(block, half_out.at[part, i, way])
+                half_copy(part, i, way).start()
+        return carry
+
+    def near_step(i, carry):
+        zz = turn(z, offset_of(i), 8)
+        for way in (0, 1):
+            for part in (0, 1):
+                half_copy(part, i, way).wait_recv()
+                block = plane_block(part, zz, 1 if way == 0 else 3)
+                block = add_half(block, way, decode(half_in.at[part, i, way]))
+                encode(block, near_out.at[part, i, way])
+                near_copy(part, i, way).start()
         return carry
 
     def item_z_copy(o):
@@ -464,7 +438,7 @@
             device(turn(z, o, 8), y, x, c),
         )
 
-    lax.fori_loop(0, 1, plane_step, 0)
+    lax.fori_loop(0, 8, half_step, 0)
     item_first.wait_recv()
     item_half[...] = item_sums[pl.ds(c * 4, 4)].reshape(512, 128) + item_in[...].reshape(512, 128)
 
@@ -475,30 +449,62 @@
         return carry
 
     lax.fori_loop(1, 8, item_step_z, 0)
-    lax.fori_loop(1, 8, plane_step, 0)
-
-    def column_copy(part, i):
+    lax.fori_loop(0, 8, near_step, 0)
+
+    def plane_total(i):
+        zz = turn(z, offset_of(i), 8)
+        for part in (0, 1):
+            for way in (0, 1):
+                near_copy(part, i, way).wait_recv()
+            value = plane_block(part, zz, 0)
+            for way in (0, 1):
+                value += decode(near_in.at[part, i, way])
+            total[part, lax.rem(i, 2)] = value
+
+    def z_where(way):
+        return device(turn(z, 1 + 6 * way, 8), y, x, c)
+
+    def far_copy(part, way):
         return copy(
-            column_out.at[part, i], column_in.at[part, i],
-            column_send.at[part, i], column_recv.at[part, i],
-            device(turn(z, offset_of(i), 8), y, x, c),
-        )
-
-    def plane_total(part, i):
-        value = plane_block(part, turn(z, offset_of(i), 8), 0)
-        for k in (1, 2, 3):
-            plane_copy(part, i, k).wait_recv()
-        for k in (1, 2, 3):
-            value += decode(plane_in.at[part, i, k - 1])
-        return value
-
-    def column_step(i, carry):
+            far_out.at[part, way], far_in.at[part, way], far_send.at[part, way], far_recv.at[part, way],
+            z_where(way),
+        )
+
+    def column_copy(part, distance, way):
+        return copy(
+            column_out.at[part, distance - 1, way], column_in.at[part, distance - 1, way],
+            column_send.at[part, distance - 1, way], column_recv.at[part, distance - 1, way],
+            z_where(way),
+        )
+
+    def far_step():
         for part in (0, 1):
-            encode(plane_total(part, i), column_out.at[part, i])
-            column_copy(part, i).start()
-        return carry
-
-    lax.fori_loop(0, 1, column_step, 0)
+            for way in (0, 1):
+                encode(total[part, 0, 128 * way:128 * way + 128], far_out.at[part, way])
+                far_copy(part, way).start()
+
+    def third_step(way):
+        for part in (0, 1):
+            far_copy(part, way).wait_recv()
+            value = add_half(total[part, 1 - way], way, decode(far_in.at[part, way]))
+            encode(value, column_out.at[part, 2, way])
+            column_copy(part, 3, way).start()
+
+    def column_step(i):
+        way = 1 - lax.rem(i, 2)
+        distance = 4 - (i + 1) // 2
+        for part in (0, 1):
+            column_copy(part, distance + 1, way).wait_recv()
+            value = total[part, lax.rem(i, 2)] + decode(column_in.at[part, distance, way])
+            encode(value, column_out.at[part, distance - 1, way])
+            column_copy(part, distance, way).start()
+
+    def both_step(i, carry):
+        plane_total(i)
+        column_step(i - 1)
+        return carry
+
+    plane_total(0)
     def item_gather(o, value):
         item_z_copy(o).wait_recv()
         return value + decode(item_z.at[o - 1])
@@ -512,7 +518,8 @@
         item_send.at[1], item_recv.at[1], pair,
     )
     item_pair.start()
-    lax.fori_loop(1, 3, column_step, 0)
+    plane_total(1)
+    far_step()
     item_pair.wait_recv()
     encode(
         item_pair_out[pl.ds(pl.multiple_of(ylo * 32, 32), 32)] + item_pair_in[...],
@@ -522,7 +529,10 @@
         item_grads.at[c, z, ylo], item_grads.at[c, z, ylo], item_send.at[2], item_recv.at[2], pair
     )
     item_share.start()
-    lax.fori_loop(3, 4, column_step, 0)
+    plane_total(2)
+    third_step(0)
+    plane_total(3)
+    third_step(1)
     item_share.wait_recv()
 
     def item_back(o):
@@ -536,9 +546,7 @@
         return carry
 
     lax.fori_loop(1, 8, item_back_start, 0)
-    lax.fori_loop(4, 7, column_step, 0)
-    for part in (0, 1):
-        total[part] = plane_total(part, 7)
+    lax.fori_loop(4, 8, both_step, 0)
 
     def item_back_wait(o, carry):
         item_back(o).wait_recv()
@@ -548,13 +556,10 @@
     item_last = copy(item_grads.at[c], item_grads.at[c], item_send.at[3], item_recv.at[3], mate)
     item_last.start()
 
-    def column_gather(i, carry):
-        for part in (0, 1):
-            column_copy(part, i).wait_recv()
-            total[part] += decode(column_in.at[part, i])
-        return carry
-
-    lax.fori_loop(0, 7, column_gather, 0)
+    for part in (0, 1):
+        for way in (0, 1):
+            column_copy(part, 1, way).wait_recv()
+            total[part, 1] += decode(column_in.at[part, 0, way])
 
     def last_rows(part, k):
         if part == 0:
@@ -562,7 +567,7 @@
             place = lax.rem(other, 2) * 2 + other // 2
         else:
             place = turn(x, k, 4)
-        return total[part, pl.ds(pl.multiple_of(place * 64, 64), 64)]
+        return total[part, 1, pl.ds(pl.multiple_of(place * 64, 64), 64)]
 
     def last_copy(part, k):
         return copy(
@@ -607,19 +612,23 @@
 
     def plane_drain(i, carry):
         for part in (0, 1):
-            for k in (1, 2, 3):
-                plane_copy(part, i, k).wait_send()
-        return carry
-
-    def column_drain(i, carry):
-        for part in (0, 1):
-            column_copy(part, i).wait_send()
-        item_z_copy(i + 1).wait_send()
-        item_back(i + 1).wait_send()
+            for way in (0, 1):
+                half_copy(part, i, way).wait_send()
+                near_copy(part, i, way).wait_send()
+        return carry
+
+    def item_drain(o, carry):
+        item_z_copy(o).wait_send()
+        item_back(o).wait_send()
         return carry
 
     lax.fori_loop(0, 8, plane_drain, 0)
-    lax.fori_loop(0, 7, column_drain, 0)
+    lax.fori_loop(1, 8, item_drain, 0)
+    for part in (0, 1):
+        for way in (0, 1):
+            far_copy(part, way).wait_send()
+            for distance in (1, 2, 3):
+                column_copy(part, distance, way).wait_send()
     for part in (0, 1):
         for k in (1, 2, 3):
             last_copy(part, k).wait_send()
@@ -645,8 +654,10 @@
     vmem = pl.BlockSpec(memory_space=pltpu.VMEM)
     dma = pltpu.SemaphoreType.DMA
     i16, f32 = jnp.int16, jnp.float32
-    plane = (2, 8, 3, 256 + SCALE_ROWS, 128)
-    column = (2, 7, 256 + SCALE_ROWS, 128)
+    half = (2, 8, 2, 128 + SCALE_ROWS, 128)
+    near = (2, 8, 2, 256 + SCALE_ROWS, 128)
+    far = (2, 2, 128 + SCALE_ROWS, 128)
+    column = (2, 3, 2, 256 + SCALE_ROWS, 128)
     last = (2, 3, 64 + SCALE_ROWS, 128)
     return pl.pallas_call(
         reduce_kernel,
@@ -654,25 +665,27 @@
             jax.ShapeDtypeStruct((1024, 128), f32),
             jax.ShapeDtypeStruct((1024, 128), f32),
         ),
-        in_specs=[pl.BlockSpec(memory_space=pltpu.HBM), vmem, vmem, vmem],
+        in_specs=[vmem, vmem, vmem, vmem],
         out_specs=(vmem, vmem),
         scratch_shapes=[
-            pltpu.VMEM((8, 2, 2, 4, 128, 128), f32),
-            pltpu.VMEM(plane, i16), pltpu.VMEM(plane, i16),
+            pltpu.VMEM(half, i16), pltpu.VMEM(half, i16),
+            pltpu.VMEM(near, i16), pltpu.VMEM(near, i16),
+            pltpu.VMEM(far, i16), pltpu.VMEM(far, i16),
             pltpu.VMEM(column, i16), pltpu.VMEM(column, i16),
-            pltpu.VMEM((2, 256, 128), f32),
+            pltpu.VMEM((2, 2, 256, 128), f32),
             pltpu.VMEM(last, i16), pltpu.VMEM(last, i16),
             pltpu.VMEM((8, 128 + SCALE_ROWS, 128), i16),
             pltpu.VMEM((4, 128, 128), f32), pltpu.VMEM((512, 128), f32),
             pltpu.VMEM((7, 64 + SCALE_ROWS, 128), i16), pltpu.VMEM((7, 64 + SCALE_ROWS, 128), i16),
             pltpu.VMEM((64, 128), f32), pltpu.VMEM((32, 128), f32),
             pltpu.VMEM((2, 8, 2, 32 + SCALE_ROWS, 128), i16),
-            dma((8,)), dma((2, 8, 3)), dma((2, 8, 3)), dma((2, 7)), dma((2, 7)),
+            dma((2, 8, 2)), dma((2, 8, 2)), dma((2, 8, 2)), dma((2, 8, 2)),
+            dma((2, 2)), dma((2, 2)), dma((2, 3, 2)), dma((2, 3, 2)),
             dma((2, 3)), dma((2, 3)), dma((7,)), dma((7,)),
             dma((4,)), dma((4,)), dma((7,)), dma((7,)), dma((7,)), dma((7,)),
         ],
         compiler_params=pltpu.CompilerParams(
-            collective_id=1, has_side_effects=True, vmem_limit_bytes=40 * 2**20
+            collective_id=1, has_side_effects=True, vmem_limit_bytes=16 * 2**20
         ),
     )(sums.reshape(8, 2, 2, 4, 128, 128), item_sums, own_users, own_items)
 
@@ -689,11 +702,11 @@
         ],
         axis=0,
     )
-    users, mate_scores, mate_lists = gather(user_factors, scores, lists)
+    users, all_scores, all_lists = gather(user_factors, scores, lists)
     core = lax.rem(lax.axis_index("user"), 2).astype(jnp.int32).reshape(1)
     user_sums, item_sums = local(
-        core, lists, mate_lists, users.reshape(128, 128, 128), item_factors.reshape(8, 128, 128),
-        scores, mate_scores,
+        core, all_lists, users.reshape(128, 128, 128), item_factors.reshape(8, 128, 128),
+        all_scores.reshape(256, 128, 128),
     )
     return reduce(user_sums, item_sums, user_factors, item_factors)
 

time: 121 us -> 98.1 us (0.81)
  Pallas kernels: 108 us -> 94.1 us
  local copies, waits for them, and re-layouts: 10.1 us -> 1.75 us
    pallas_call x1, Pallas kernels: 64.1 us -> 49.6 us  [reduce(): pl.pallas_call(reduce_kernel, out_shape=(jax.ShapeDtypeStruct((1024, 128)...]
    unnamed x14 -> x6, local copies, waits for them, and re-layouts: 9.92 us -> 1.6 us
where the time goes in v2:
time: 98.1 us; the launch traced here: 98 us
  Pallas kernels  94.1 us (96%)
  local copies, waits for them, and re-layouts  1.75 us (2%)
  between operations  1.38 us (1%)
    pallas_call x1, Pallas kernels, reduce(): pl.pallas_call(reduce_kernel, out_shape=(jax.ShapeDtypeStruct((1024, 128)...  49.6 us
    pallas_call x1, Pallas kernels, gather(): pl.pallas_call(functools.partial(gather_kernel, (ROWS_A, ROWS_B, ROWS_C))...  36.9 us
    pallas_call x1, Pallas kernels, local(): pl.pallas_call(local_kernel, out_shape=(jax.ShapeDtypeStruct((128, 128, 1...  7.68 us

profile of v2, /device:TPU:6, one launch (start us, length us, event | category | flops | bytes accessed | tf_op | source)
XLA Modules:
  0.0 98.0 jit_solution(15630901554912734344)
XLA Ops:
  0.6 0.0 copy-start
  1.3 0.1 pad.2.clone
  1.4 0.1 pad.3.clone
  1.5 0.7 add_add_fusion.lists
  2.2 36.9 %shard_map.77 = (bf16[8,2,2,4,128,128]{5,4,3,2,1,0:T(8,128)(2,1)S(1)}, s32[2,128,128,128]{3,2,1,0:T(8,128)S(1)}, s32[2,8,128]{2,1,0:T(8,128)S(1)}) custom-call(bf16[2,4,128,128]{3,2,1,0:T(8,128)(2,1)} %bitcast.17, s32[128,128,128]{2,1,0:T(8,128)} %bitcast.18, s32[8,128]{1,0:T(8,128)S(1)} %add_add_fusion.lists), custom_call_target="tpu_custom_call" | custom-call | tf_op jit(solution)/shard_map/pallas_call | solution.py:214
  39.1 0.0 copy-done
  39.1 0.0 copy-start.1
  39.1 7.7 %shard_map.78 = (f32[128,128,128]{2,1,0:T(8,128)S(1)}, f32[8,128,128]{2,1,0:T(8,128)S(1)}) custom-call(s32[1]{0:T(128)} %bitcast.core, s32[2,8,128]{2,1,0:T(8,128)S(1)} %get-tuple-element.7.lists, bf16[128,128,128]{2,1,0:T(8,128)(2,1)S(1)} %bitcast.15, bf16[8,128,128]{2,1,0:T(8,128)(2,1)S(1)} %bitcast.16, s32[256,128,128]{2,1,0:T(8,128)S(1)} %bitcast.13), custom_call_target="tpu_custom_call" | custom-call | tf_op jit(solution)/shard_map/pallas_call | solution.py:311
  46.8 0.0 copy-done.1
  46.8 49.6 %shard_map.79 = (f32[1024,128]{1,0:T(8,128)S(1)}, f32[1024,128]{1,0:T(8,128)S(1)}) custom-call(f32[8,2,2,4,128,128]{5,4,3,2,1,0:T(8,128)S(1)} %bitcast.14, f32[8,128,128]{2,1,0:T(8,128)S(1)} %get-tuple-element.11.item_sums, bf16[1024,128]{1,0:T(8,128)(2,1)S(1)} %copy-done.1, bf16[1024,128]{1,0:T(8,128)(2,1)S(1)} %copy-done), custom_call_target="tpu_custom_call" | custom-call | tf_op jit(solution)/shard_map/pallas_call | solution.py:662
  96.4 0.8 copy.11
  97.2 0.8 copy.12
  (1 shorter events, 0.0 us)
Async XLA Ops:
  0.6 38.5 %copy-start = (bf16[1024,128]{1,0:T(8,128)(2,1)S(1)}, bf16[1024,128]{1,0:T(8,128)(2,1)}, u32[]{:S(2)}) copy-start(bf16[1024,128]{1,0:T(8,128)(2,1)} %own_items.1) | copy-start | bytes 786436
  39.1 7.7 %copy-start.1 = (bf16[1024,128]{1,0:T(8,128)(2,1)S(1)}, bf16[1024,128]{1,0:T(8,128)(2,1)}, u32[]{:S(2)}) copy-start(bf16[1024,128]{1,0:T(8,128)(2,1)} %own_users.1) | copy-start | bytes 786436

commit v3 on v2

--- a/solution.py
+++ b/solution.py
@@ -65,11 +65,11 @@
             copy.wait_send()
 
 
-ROWS_A, ROWS_B, ROWS_C = 64, 32, 32
+ROWS_A, ROWS_B, ROWS_C = 48, 48, 32
 GATHER_COPIES = 160
 
 
-def gather_kernel(split, own, ratings, lists, users, all_ratings, all_lists, local_sems, send_sems, recv_sems):
+def gather_kernel(split, own, ratings, lists, users, all_ratings, all_lists, no_users, no_items, local_sems, send_sems, recv_sems):
     z, ylo, yhi, x, c = here()
     y = yhi * 2 + ylo
     near = neighbours()
@@ -126,19 +126,36 @@
         block = part_a(zed(offset), ylo, x)
         pair[offset] = send(block, block, near["pair"])
 
+    late = (-3, 3, 4)
+
+    def direct(block, where):
+        last.append(send(block, block, where))
+
     def x_send(offset, low):
-        if offset == 0 and low == 0:
+        if offset == 0 and low == 0 or offset == 4 and low == 1:
+            return
+        if offset in late:
+            block = part_a(zed(offset), ylo if low == 0 else 1 - ylo, x)
+            rows = (y, yhi * 2 + 1 - ylo) if offset == 4 else (y,)
+            for k in (2, 1, 3):
+                for row in rows:
+                    direct(block, device(z, row, lax.rem(x + k, 4), c))
             return
         block = part_a(zed(offset), ylo if low == 0 else 1 - ylo, x)
         first["x", offset, low] = [send(block, block, near["x"][way]) for way in (0, 1)]
 
     def y_send(offset):
+        if offset in late:
+            block = part_b(zed(offset), y)
+            for k in (2, 1, 3):
+                direct(block, device(z, lax.rem(y + k, 4), x, c))
+            return
         block = part_b(zed(offset), y)
         first["y", offset, 0] = [send(block, block, near["y"][way]) for way in (0, 1)]
 
     def forward(axis, offset, low):
         zz = zed(offset)
-        if axis == "x" and offset == 0 and low == 0:
+        if axis == "x" and offset == 0 and low == 0 or offset in late:
             return
         for way in (0, 1):
             first[axis, offset, low][way].wait_recv()
@@ -155,11 +172,18 @@
     z_send("B", 1)
     pair_c = send(part_c(z, ylo), part_c(z, ylo), near["pair"])
     pair_send(0)
+    z_send("C", 1)
     x_send(0, 0)
     y_send(0)
-    z_send("C", 1)
     far = send(ratings, all_ratings.at[c], near["mate"])
     far_lists = send(lists, all_lists.at[c], near["mate"])
+    no_items[...] = jnp.zeros_like(no_items)
+
+    def clear(k, carry):
+        no_users[k] = jnp.zeros(no_users.shape[1:], jnp.float32)
+        return carry
+
+    lax.fori_loop(0, no_users.shape[0], clear, 0)
     before = [0]
     for step in (1, 2, 3, 4):
         offsets = [-step, step] if step < 4 else [4]
@@ -217,6 +241,8 @@
             jax.ShapeDtypeStruct((8, 2, 2, 4, 128, 128), jnp.bfloat16),
             jax.ShapeDtypeStruct((2, *ratings.shape), jnp.int32),
             jax.ShapeDtypeStruct((2, *lists.shape), jnp.int32),
+            jax.ShapeDtypeStruct((128, 128, 128), jnp.float32),
+            jax.ShapeDtypeStruct((8, 128, 128), jnp.float32),
         ),
         in_specs=[
             pl.BlockSpec(memory_space=pltpu.HBM),
@@ -226,6 +252,8 @@
         out_specs=(
             pl.BlockSpec(memory_space=space),
             pl.BlockSpec(memory_space=space),
+            pl.BlockSpec(memory_space=pltpu.VMEM),
+            pl.BlockSpec(memory_space=pltpu.VMEM),
             pl.BlockSpec(memory_space=pltpu.VMEM),
         ),
         scratch_shapes=[
@@ -246,9 +274,8 @@
 GROUP = 16
 
 
-def local_kernel(core, lists, users, items, ratings, user_sum, item_sum, order):
+def local_kernel(core, lists, users, items, ratings, no_users, no_items, user_sum, item_sum, order):
     mine = core[0]
-    edge = ratings.shape[1]
 
     def scan(table):
         def visit(slot, count):
@@ -262,13 +289,6 @@
     count = lax.fori_loop(0, lists[1, 2, 0], scan(1), count)
     for k in range(GROUP):
         order[count + k] = 0
-
-    def clear(k, carry):
-        user_sum[k] = jnp.zeros((edge, 128), jnp.float32)
-        return carry
-
-    lax.fori_loop(0, 128, clear, 0)
-    item_sum[...] = jnp.zeros_like(item_sum)
 
     def step(g, carry):
         first = g * GROUP
@@ -305,7 +325,7 @@
     lax.fori_loop(0, (count + GROUP - 1) // GROUP, step, 0)
 
 
-def local(core, lists, users, items, ratings):
+def local(core, lists, users, items, ratings, no_users, no_items):
     smem = pl.BlockSpec(memory_space=pltpu.SMEM)
     vmem = pl.BlockSpec(memory_space=pltpu.VMEM)
     return pl.pallas_call(
@@ -314,11 +334,12 @@
             jax.ShapeDtypeStruct((128, 128, 128), jnp.float32),
             jax.ShapeDtypeStruct((8, 128, 128), jnp.float32),
         ),
-        in_specs=[smem, smem, vmem, vmem, vmem],
+        in_specs=[smem, smem, vmem, vmem, vmem, vmem, vmem],
         out_specs=(vmem, vmem),
+        input_output_aliases={5: 0, 6: 1},
         scratch_shapes=[pltpu.SMEM((256 + GROUP,), jnp.int32)],
         compiler_params=pltpu.CompilerParams(vmem_limit_bytes=8 * 2**20),
-    )(core, lists, users, items, ratings)
+    )(core, lists, users, items, ratings, no_users, no_items)
 
 
 user_step = 0.1
@@ -546,7 +567,9 @@
         return carry
 
     lax.fori_loop(1, 8, item_back_start, 0)
-    lax.fori_loop(4, 8, both_step, 0)
+    lax.fori_loop(4, 7, both_step, 0)
+    column_step(6)
+    plane_total(7)
 
     def item_back_wait(o, carry):
         item_back(o).wait_recv()
@@ -702,11 +725,11 @@
         ],
         axis=0,
     )
-    users, all_scores, all_lists = gather(user_factors, scores, lists)
+    users, all_scores, all_lists, no_users, no_items = gather(user_factors, scores, lists)
     core = lax.rem(lax.axis_index("user"), 2).astype(jnp.int32).reshape(1)
     user_sums, item_sums = local(
         core, all_lists, users.reshape(128, 128, 128), item_factors.reshape(8, 128, 128),
-        all_scores.reshape(256, 128, 128),
+        all_scores.reshape(256, 128, 128), no_users, no_items,
     )
     return reduce(user_sums, item_sums, user_factors, item_factors)
 

time: 98.1 us -> 93.9 us (0.957)
  Pallas kernels: 94.1 us -> 90 us
    pallas_call x1, Pallas kernels: 7.68 us -> 3.28 us  [local(): pl.pallas_call(local_kernel, out_shape=(jax.ShapeDtypeStruct((128, 128, 1...]
    pallas_call x1, Pallas kernels: 49.6 us -> 52.5 us  [reduce(): pl.pallas_call(reduce_kernel, out_shape=(jax.ShapeDtypeStruct((1024, 128)...]
    pallas_call x1, Pallas kernels: 36.9 us -> 34.2 us  [gather(): pl.pallas_call(functools.partial(gather_kernel, (ROWS_A, ROWS_B, ROWS_C))...]
where the time goes in v3:
time: 93.9 us; the launch traced here: 93.8 us
  Pallas kernels  90 us (96%)
  local copies, waits for them, and re-layouts  1.75 us (2%)
  between operations  1.38 us (1%)
    pallas_call x1, Pallas kernels, reduce(): pl.pallas_call(reduce_kernel, out_shape=(jax.ShapeDtypeStruct((1024, 128)...  52.5 us
    pallas_call x1, Pallas kernels, gather(): pl.pallas_call(functools.partial(gather_kernel, (ROWS_A, ROWS_B, ROWS_C))...  34.2 us
    pallas_call x1, Pallas kernels, local(): pl.pallas_call(local_kernel, out_shape=(jax.ShapeDtypeStruct((128, 128, 1...  3.28 us

profile of v3, /device:TPU:6, one launch (start us, length us, event | category | flops | bytes accessed | tf_op | source)
XLA Modules:
  0.0 93.8 jit_solution(2718611748135184076)
XLA Ops:
  0.6 0.0 copy-start
  1.3 0.1 pad.2.clone
  1.4 0.1 pad.3.clone
  1.5 0.7 add_add_fusion.lists
  2.2 34.2 %shard_map.77 = (bf16[8,2,2,4,128,128]{5,4,3,2,1,0:T(8,128)(2,1)S(1)}, s32[2,128,128,128]{3,2,1,0:T(8,128)S(1)}, s32[2,8,128]{2,1,0:T(8,128)S(1)}, f32[128,128,128]{2,1,0:T(8,128)S(1)}, f32[8,128,128]{2,1,0:T(8,128)S(1)}) custom-call(bf16[2,4,128,128]{3,2,1,0:T(8,128)(2,1)} %bitcast.17, s32[128,128,128]{2,1,0:T(8,128)} %bitcast.18, ...), custom_call_target="tpu_custom_call" | custom-call | tf_op jit(solution)/shard_map/pallas_call | solution.py:238
  36.4 0.0 copy-done
  36.4 0.0 copy-start.1
  36.5 3.3 %shard_map.78 = (f32[128,128,128]{2,1,0:T(8,128)S(1)}, f32[8,128,128]{2,1,0:T(8,128)S(1)}) custom-call(s32[1]{0:T(128)} %bitcast.core, s32[2,8,128]{2,1,0:T(8,128)S(1)} %get-tuple-element.9.lists, bf16[128,128,128]{2,1,0:T(8,128)(2,1)S(1)} %bitcast.15, bf16[8,128,128]{2,1,0:T(8,128)(2,1)S(1)} %bitcast.16, ...), custom_call_target="tpu_custom_call", output_to_operand_aliasing={{0}: (5, {}), {1}: (6, {})} | custom-call | tf_op jit(solution)/shard_map/pallas_call | solution.py:331
  39.7 0.0 copy-done.1
  39.8 52.5 %shard_map.79 = (f32[1024,128]{1,0:T(8,128)S(1)}, f32[1024,128]{1,0:T(8,128)S(1)}) custom-call(f32[8,2,2,4,128,128]{5,4,3,2,1,0:T(8,128)S(1)} %bitcast.13, f32[8,128,128]{2,1,0:T(8,128)S(1)} %get-tuple-element.15.item_sums, bf16[1024,128]{1,0:T(8,128)(2,1)S(1)} %copy-done.1, bf16[1024,128]{1,0:T(8,128)(2,1)S(1)} %copy-done), custom_call_target="tpu_custom_call" | custom-call | tf_op jit(solution)/shard_map/pallas_call | solution.py:685
  92.3 0.8 copy.15
  93.1 0.8 copy.16
  (1 shorter events, 0.0 us)
Async XLA Ops:
  0.6 35.8 %copy-start = (bf16[1024,128]{1,0:T(8,128)(2,1)S(1)}, bf16[1024,128]{1,0:T(8,128)(2,1)}, u32[]{:S(2)}) copy-start(bf16[1024,128]{1,0:T(8,128)(2,1)} %own_items.1) | copy-start | bytes 786436
  36.4 3.3 %copy-start.1 = (bf16[1024,128]{1,0:T(8,128)(2,1)S(1)}, bf16[1024,128]{1,0:T(8,128)(2,1)}, u32[]{:S(2)}) copy-start(bf16[1024,128]{1,0:T(8,128)(2,1)} %own_users.1) | copy-start | bytes 786436

commit v4 on v3

--- a/solution.py
+++ b/solution.py
@@ -345,7 +345,12 @@
 user_step = 0.1
 item_step = 0.04
 shrinkage = 0.1
-SCALE_ROWS = 16
+EDGE_ROWS, MIDDLE_ROWS = 56, 16
+CHUNK = 4 * EDGE_ROWS
+
+
+def coded_rows(rows):
+    return rows + (16 if rows % 16 == 0 else 8)
 
 
 def encode(value, buffer):
@@ -354,24 +359,28 @@
     peak = jnp.maximum(jnp.max(jnp.abs(folded), axis=0), 1e-30)
     power = jnp.ceil(jnp.log2(peak))
     whole = jnp.round(folded * jnp.exp2(14.0 - power)).reshape(rows, 128)
-    buffer[0:rows] = whole.astype(jnp.int32).astype(jnp.int16)
-    both = jnp.concatenate([power, power], axis=0)
-    buffer[rows:rows + SCALE_ROWS] = both.astype(jnp.int32).astype(jnp.int16)
-
-
-def decode(buffer):
-    rows = buffer.shape[0] - SCALE_ROWS
-    power = buffer[rows:rows + SCALE_ROWS].astype(jnp.float32)[0:8]
-    folded = buffer[0:rows].astype(jnp.float32).reshape(rows // 8, 8, 128)
+    tail = [power] * ((coded_rows(rows) - rows) // 8)
+    buffer[...] = jnp.concatenate([whole, *tail], axis=0).astype(jnp.int32).astype(jnp.int16)
+
+
+def decode(buffer, rows):
+    every = coded_rows(rows)
+    power = buffer[every - 16:every].astype(jnp.float32)[8:16]
+    folded = buffer[...].astype(jnp.float32)[0:rows].reshape(rows // 8, 8, 128)
     return (folded * jnp.exp2(power - 14.0)).reshape(rows, 128)
 
 
 def reduce_kernel(
     sums, item_sums, own_users, own_items, new_users, new_items,
-    half_out, half_in, near_out, near_in, far_out, far_in, column_out, column_in, total, last_out, last_in, grads,
-    item_in, item_half, item_out, item_z, item_pair_out, item_pair_in, item_grads,
-    half_send, half_recv, near_send, near_recv, far_send, far_recv, column_send, column_recv, last_send, last_recv,
-    grad_send, grad_recv, item_send, item_recv, item_z_send, item_z_recv, item_back_send, item_back_recv,
+    half_out, half_in, near_out, near_in, far_out, far_in, column_out, column_in, total,
+    last_out, last_in, grads,
+    mid_far_out, mid_far_in, mid_out, mid_in, mid_total, mid_y_out, mid_y_in, mid_row, mid_x_out, mid_x_in, mid_grads,
+    item_in, item_half, item_pair_out, item_pair_in, item_row, item_out, item_z, item_grads,
+    half_send, half_recv, near_send, near_recv, far_send, far_recv, column_send, column_recv,
+    last_send, last_recv, grad_send, grad_recv,
+    mid_far_send, mid_far_recv, mid_send, mid_recv, mid_y_send, mid_y_recv, mid_x_send, mid_x_recv,
+    mid_grad_send, mid_grad_recv,
+    item_send, item_recv, item_z_send, item_z_recv, item_back_send, item_back_recv,
 ):
     z, ylo, yhi, x, c = here()
     y = yhi * 2 + ylo
@@ -390,10 +399,9 @@
         return 4 + (1 - 2 * lax.rem(i, 2)) * ((i + 1) // 2)
 
     barrier = pltpu.get_barrier_semaphore()
-    others = [device(z, y, turn(x, k, 4), c) for k in (1, 2, 3)]
-    others += [device(z, turn(y, k, 4), x, c) for k in (1, 2, 3)]
-    others += [device(z, turn(y, 2, 4), turn(x, k, 4), c) for k in (1, 2, 3)]
-    others += [device(turn(z, k, 8), y, x, c) for k in range(1, 8)]
+    others = [device(z, y, turn(x, k, 4), c) for k in (1, 3)]
+    others += [device(z, turn(y, k, 4), x, c) for k in (1, 3)]
+    others += [device(turn(z, k, 8), y, x, c) for k in (1, 7)]
     others += [device(z, y, x, 1 - c)]
     for other in others:
         pl.semaphore_signal(barrier, inc=1, device_id=other, device_id_type=MESH)
@@ -409,9 +417,9 @@
 
     def plane_block(part, zz, k):
         if part == 0:
-            return sums[zz, :, :, turn(x, k, 4), 0:64].reshape(256, 128)
+            return sums[zz, :, :, turn(x, k, 4), 0:EDGE_ROWS].reshape(CHUNK, 128)
         other = turn(y, k, 4)
-        return sums[zz, lax.rem(other, 2), other // 2, :, 64:128].reshape(256, 128)
+        return sums[zz, lax.rem(other, 2), other // 2, :, EDGE_ROWS:2 * EDGE_ROWS].reshape(CHUNK, 128)
 
     def toward(part, way):
         return plane_where(part, 1 if way == 0 else 3)
@@ -429,15 +437,16 @@
         )
 
     def add_half(value, way, extra):
+        split = value.shape[0] // 2
         if way == 0:
-            return jnp.concatenate([value[0:128] + extra, value[128:256]], axis=0)
-        return jnp.concatenate([value[0:128], value[128:256] + extra], axis=0)
+            return jnp.concatenate([value[0:split] + extra, value[split:]], axis=0)
+        return jnp.concatenate([value[0:split], value[split:] + extra], axis=0)
 
     def half_step(i, carry):
         zz = turn(z, offset_of(i), 8)
         for way in (0, 1):
             for part in (0, 1):
-                block = plane_block(part, zz, 2)[128 * way:128 * way + 128]
+                block = plane_block(part, zz, 2)[CHUNK // 2 * way:CHUNK // 2 * (way + 1)]
                 encode(block, half_out.at[part, i, way])
                 half_copy(part, i, way).start()
         return carry
@@ -448,29 +457,10 @@
             for part in (0, 1):
                 half_copy(part, i, way).wait_recv()
                 block = plane_block(part, zz, 1 if way == 0 else 3)
-                block = add_half(block, way, decode(half_in.at[part, i, way]))
+                block = add_half(block, way, decode(half_in.at[part, i, way], CHUNK // 2))
                 encode(block, near_out.at[part, i, way])
                 near_copy(part, i, way).start()
         return carry
-
-    def item_z_copy(o):
-        return copy(
-            item_out.at[o - 1], item_z.at[o - 1], item_z_send.at[o - 1], item_z_recv.at[o - 1],
-            device(turn(z, o, 8), y, x, c),
-        )
-
-    lax.fori_loop(0, 8, half_step, 0)
-    item_first.wait_recv()
-    item_half[...] = item_sums[pl.ds(c * 4, 4)].reshape(512, 128) + item_in[...].reshape(512, 128)
-
-    def item_step_z(o, carry):
-        zz = turn(z, o, 8)
-        encode(item_half[pl.ds(pl.multiple_of(zz * 64, 64), 64)], item_out.at[o - 1])
-        item_z_copy(o).start()
-        return carry
-
-    lax.fori_loop(1, 8, item_step_z, 0)
-    lax.fori_loop(0, 8, near_step, 0)
 
     def plane_total(i):
         zz = turn(z, offset_of(i), 8)
@@ -479,7 +469,7 @@
                 near_copy(part, i, way).wait_recv()
             value = plane_block(part, zz, 0)
             for way in (0, 1):
-                value += decode(near_in.at[part, i, way])
+                value += decode(near_in.at[part, i, way], CHUNK)
             total[part, lax.rem(i, 2)] = value
 
     def z_where(way):
@@ -501,13 +491,13 @@
     def far_step():
         for part in (0, 1):
             for way in (0, 1):
-                encode(total[part, 0, 128 * way:128 * way + 128], far_out.at[part, way])
+                encode(total[part, 0, CHUNK // 2 * way:CHUNK // 2 * (way + 1)], far_out.at[part, way])
                 far_copy(part, way).start()
 
     def third_step(way):
         for part in (0, 1):
             far_copy(part, way).wait_recv()
-            value = add_half(total[part, 1 - way], way, decode(far_in.at[part, way]))
+            value = add_half(total[part, 1 - way], way, decode(far_in.at[part, way], CHUNK // 2))
             encode(value, column_out.at[part, 2, way])
             column_copy(part, 3, way).start()
 
@@ -516,7 +506,7 @@
         distance = 4 - (i + 1) // 2
         for part in (0, 1):
             column_copy(part, distance + 1, way).wait_recv()
-            value = total[part, lax.rem(i, 2)] + decode(column_in.at[part, distance, way])
+            value = total[part, lax.rem(i, 2)] + decode(column_in.at[part, distance, way], CHUNK)
             encode(value, column_out.at[part, distance - 1, way])
             column_copy(part, distance, way).start()
 
@@ -525,64 +515,157 @@
         column_step(i - 1)
         return carry
 
-    plane_total(0)
-    def item_gather(o, value):
-        item_z_copy(o).wait_recv()
-        return value + decode(item_z.at[o - 1])
-
-    item_total = lax.fori_loop(
-        1, 8, item_gather, item_half[pl.ds(pl.multiple_of(z * 64, 64), 64)]
+    def mid_block(zz):
+        return sums[zz, :, :, :, 2 * EDGE_ROWS:128].reshape(16 * MIDDLE_ROWS, 128)
+
+    def mid_far_copy(way):
+        return copy(
+            mid_far_out.at[way], mid_far_in.at[way], mid_far_send.at[way], mid_far_recv.at[way], z_where(way)
+        )
+
+    def mid_copy(distance, way):
+        return copy(
+            mid_out.at[distance - 1, way], mid_in.at[distance - 1, way],
+            mid_send.at[distance - 1, way], mid_recv.at[distance - 1, way], z_where(way),
+        )
+
+    def mid_far():
+        for way in (0, 1):
+            block = mid_block(turn(z, 4, 8))[8 * MIDDLE_ROWS * way:8 * MIDDLE_ROWS * (way + 1)]
+            encode(block, mid_far_out.at[way])
+            mid_far_copy(way).start()
+
+    def mid_step(distance):
+        for way in (0, 1):
+            block = mid_block(turn(z, distance if way == 0 else 8 - distance, 8))
+            if distance == 3:
+                mid_far_copy(way).wait_recv()
+                block = add_half(block, way, decode(mid_far_in.at[way], 8 * MIDDLE_ROWS))
+            else:
+                mid_copy(distance + 1, way).wait_recv()
+                block += decode(mid_in.at[distance, way], 16 * MIDDLE_ROWS)
+            encode(block, mid_out.at[distance - 1, way])
+            mid_copy(distance, way).start()
+
+    def mid_y_copy(k):
+        return copy(
+            mid_y_out.at[k - 1], mid_y_in.at[k - 1], mid_y_send.at[k - 1], mid_y_recv.at[k - 1],
+            plane_where(1, k),
+        )
+
+    def mid_x_copy(k):
+        return copy(
+            mid_x_out.at[k - 1], mid_x_in.at[k - 1], mid_x_send.at[k - 1], mid_x_recv.at[k - 1],
+            plane_where(0, k),
+        )
+
+    def mid_y_rows(k):
+        other = turn(y, k, 4)
+        place = lax.rem(other, 2) * 2 + other // 2
+        size = 4 * MIDDLE_ROWS
+        return mid_total[pl.ds(pl.multiple_of(place * size, size), size)]
+
+    def mid_x_rows(k):
+        return mid_row[pl.ds(pl.multiple_of(turn(x, k, 4) * MIDDLE_ROWS, MIDDLE_ROWS), MIDDLE_ROWS)]
+
+    def mid_to_y():
+        value = mid_block(z)
+        for way in (0, 1):
+            mid_copy(1, way).wait_recv()
+            value += decode(mid_in.at[0, way], 16 * MIDDLE_ROWS)
+        mid_total[...] = value
+        for k in (2, 1, 3):
+            encode(mid_y_rows(k), mid_y_out.at[k - 1])
+            mid_y_copy(k).start()
+
+    def mid_to_x():
+        value = mid_y_rows(0)
+        for k in (1, 2, 3):
+            mid_y_copy(k).wait_recv()
+            value += decode(mid_y_in.at[k - 1], 4 * MIDDLE_ROWS)
+        mid_row[...] = value
+        for k in (2, 1, 3):
+            encode(mid_x_rows(k), mid_x_out.at[k - 1])
+            mid_x_copy(k).start()
+
+    def q_where(m):
+        other = turn(q, m, 8)
+        return device(z, (other // 4) * 2 + ylo, lax.rem(other, 4), c)
+
+    def mid_grad_copy(m):
+        return copy(
+            mid_grads.at[q], mid_grads.at[q], mid_grad_send.at[m - 1], mid_grad_recv.at[m - 1], q_where(m)
+        )
+
+    def mid_finish():
+        value = mid_x_rows(0)
+        for k in (1, 2, 3):
+            mid_x_copy(k).wait_recv()
+            value += decode(mid_x_in.at[k - 1], MIDDLE_ROWS)
+        encode(value, mid_grads.at[q])
+        for m in range(1, 8):
+            mid_grad_copy(m).start()
+
+    item_pair = copy(item_pair_out, item_pair_in, item_send.at[1], item_recv.at[1], pair)
+
+    def item_to_pair():
+        item_first.wait_recv()
+        item_half[...] = item_sums[pl.ds(c * 4, 4)].reshape(512, 128) + item_in[...].reshape(512, 128)
+        encode(item_half[pl.ds(pl.multiple_of((1 - ylo) * 256, 256), 256)], item_pair_out)
+        item_pair.start()
+
+    def item_z_copy(o):
+        return copy(
+            item_out.at[o - 1], item_z.at[o - 1], item_z_send.at[o - 1], item_z_recv.at[o - 1],
+            device(turn(z, o, 8), y, x, c),
+        )
+
+    def item_rows(zz):
+        return item_row[pl.ds(pl.multiple_of(zz * 32, 32), 32)]
+
+    def item_to_z():
+        item_pair.wait_recv()
+        own = item_half[pl.ds(pl.multiple_of(ylo * 256, 256), 256)]
+        item_row[...] = own + decode(item_pair_in, 256)
+
+        def each(o, carry):
+            encode(item_rows(turn(z, o, 8)), item_out.at[o - 1])
+            item_z_copy(o).start()
+            return carry
+
+        lax.fori_loop(1, 8, each, 0)
+
+    def item_back(o):
+        return copy(
+            item_grads.at[c, ylo, z], item_grads.at[c, ylo, z], item_back_send.at[o - 1], item_back_recv.at[o - 1],
+            device(turn(z, o, 8), y, x, c),
+        )
+
+    def item_total():
+        def each(o, value):
+            item_z_copy(o).wait_recv()
+            return value + decode(item_z.at[o - 1], 32)
+
+        encode(lax.fori_loop(1, 8, each, item_rows(z)), item_grads.at[c, ylo, z])
+
+        def start(o, carry):
+            item_back(o).start()
+            return carry
+
+        lax.fori_loop(1, 8, start, 0)
+
+    item_share = copy(
+        item_grads.at[c, ylo], item_grads.at[c, ylo], item_send.at[2], item_recv.at[2], pair
     )
-    item_pair_out[...] = item_total
-    item_pair = copy(
-        item_pair_out.at[pl.ds(pl.multiple_of((1 - ylo) * 32, 32), 32)], item_pair_in,
-        item_send.at[1], item_recv.at[1], pair,
-    )
-    item_pair.start()
-    plane_total(1)
-    far_step()
-    item_pair.wait_recv()
-    encode(
-        item_pair_out[pl.ds(pl.multiple_of(ylo * 32, 32), 32)] + item_pair_in[...],
-        item_grads.at[c, z, ylo],
-    )
-    item_share = copy(
-        item_grads.at[c, z, ylo], item_grads.at[c, z, ylo], item_send.at[2], item_recv.at[2], pair
-    )
-    item_share.start()
-    plane_total(2)
-    third_step(0)
-    plane_total(3)
-    third_step(1)
-    item_share.wait_recv()
-
-    def item_back(o):
-        return copy(
-            item_grads.at[c, z], item_grads.at[c, z], item_back_send.at[o - 1], item_back_recv.at[o - 1],
-            device(turn(z, o, 8), y, x, c),
-        )
-
-    def item_back_start(o, carry):
-        item_back(o).start()
-        return carry
-
-    lax.fori_loop(1, 8, item_back_start, 0)
-    lax.fori_loop(4, 7, both_step, 0)
-    column_step(6)
-    plane_total(7)
-
-    def item_back_wait(o, carry):
-        item_back(o).wait_recv()
-        return carry
-
-    lax.fori_loop(1, 8, item_back_wait, 0)
     item_last = copy(item_grads.at[c], item_grads.at[c], item_send.at[3], item_recv.at[3], mate)
-    item_last.start()
-
-    for part in (0, 1):
-        for way in (0, 1):
-            column_copy(part, 1, way).wait_recv()
-            total[part, 1] += decode(column_in.at[part, 0, way])
+
+    def item_to_share():
+        def each(o, carry):
+            item_back(o).wait_recv()
+            return carry
+
+        lax.fori_loop(1, 8, each, 0)
+        item_share.start()
 
     def last_rows(part, k):
         if part == 0:
@@ -590,7 +673,7 @@
             place = lax.rem(other, 2) * 2 + other // 2
         else:
             place = turn(x, k, 4)
-        return total[part, 1, pl.ds(pl.multiple_of(place * 64, 64), 64)]
+        return total[part, 1, pl.ds(pl.multiple_of(place * EDGE_ROWS, 8), EDGE_ROWS)]
 
     def last_copy(part, k):
         return copy(
@@ -598,40 +681,54 @@
             last_send.at[part, k - 1], last_recv.at[part, k - 1], plane_where(1 - part, k),
         )
 
+    def grad_copy(m):
+        return copy(grads.at[q], grads.at[q], grad_send.at[m - 1], grad_recv.at[m - 1], q_where(m))
+
+    mid_far()
+    lax.fori_loop(0, 8, half_step, 0)
+    item_to_pair()
+    mid_step(3)
+    lax.fori_loop(0, 4, near_step, 0)
+    mid_step(2)
+    lax.fori_loop(4, 8, near_step, 0)
+    plane_total(0)
+    mid_step(1)
+    plane_total(1)
+    far_step()
+    plane_total(2)
+    third_step(0)
+    mid_to_y()
+    plane_total(3)
+    third_step(1)
+    item_to_z()
+    lax.fori_loop(4, 6, both_step, 0)
+    mid_to_x()
+    both_step(6, 0)
+    column_step(6)
+    item_total()
+    mid_finish()
+    plane_total(7)
+    for part in (0, 1):
+        for way in (0, 1):
+            column_copy(part, 1, way).wait_recv()
+            total[part, 1] += decode(column_in.at[part, 0, way], CHUNK)
     for k in (2, 1, 3):
         for part in (0, 1):
             encode(last_rows(part, k), last_out.at[part, k - 1])
             last_copy(part, k).start()
-
-    item_last.wait_recv()
-
-    def item_finish(n, carry):
-        grad = decode(item_grads.at[n // 16, lax.rem(n // 2, 8), lax.rem(n, 2)])
-        rows = pl.ds(pl.multiple_of(n * 32, 32), 32)
-        now = own_items[rows].astype(jnp.float32)
-        new_items[rows] = now - item_step * (grad + shrinkage * now)
-        return carry
-
-    lax.fori_loop(0, 32, item_finish, 0)
-
+    item_to_share()
     halves = []
     for part in (0, 1):
         value = last_rows(part, 0)
         for k in (1, 2, 3):
             last_copy(part, k).wait_recv()
-            value += decode(last_in.at[part, k - 1])
+            value += decode(last_in.at[part, k - 1], EDGE_ROWS)
         halves.append(value)
     encode(jnp.concatenate(halves, axis=0), grads.at[q])
-
-    def grad_copy(m):
-        other = turn(q, m, 8)
-        return copy(
-            grads.at[q], grads.at[q], grad_send.at[m - 1], grad_recv.at[m - 1],
-            device(z, (other // 4) * 2 + ylo, lax.rem(other, 4), c),
-        )
-
     for m in range(1, 8):
         grad_copy(m).start()
+    item_share.wait_recv()
+    item_last.start()
 
     def plane_drain(i, carry):
         for part in (0, 1):
@@ -640,29 +737,46 @@
                 near_copy(part, i, way).wait_send()
         return carry
 
-    def item_drain(o, carry):
+    def peer_drain(o, carry):
         item_z_copy(o).wait_send()
         item_back(o).wait_send()
+        mid_grad_copy(o).wait_send()
         return carry
 
     lax.fori_loop(0, 8, plane_drain, 0)
-    lax.fori_loop(1, 8, item_drain, 0)
-    for part in (0, 1):
-        for way in (0, 1):
+    lax.fori_loop(1, 8, peer_drain, 0)
+    for way in (0, 1):
+        mid_far_copy(way).wait_send()
+        for part in (0, 1):
             far_copy(part, way).wait_send()
-            for distance in (1, 2, 3):
+        for distance in (1, 2, 3):
+            mid_copy(distance, way).wait_send()
+            for part in (0, 1):
                 column_copy(part, distance, way).wait_send()
-    for part in (0, 1):
-        for k in (1, 2, 3):
+    for k in (1, 2, 3):
+        mid_y_copy(k).wait_send()
+        mid_x_copy(k).wait_send()
+        for part in (0, 1):
             last_copy(part, k).wait_send()
-    for early in (item_first, item_pair, item_share, item_last):
-        early.wait_send()
-
+    item_last.wait_recv()
+
+    def item_finish(n, carry):
+        grad = decode(item_grads.at[n // 16, lax.rem(n // 8, 2), lax.rem(n, 8)], 32)
+        rows = pl.ds(pl.multiple_of(n * 32, 32), 32)
+        now = own_items[rows].astype(jnp.float32)
+        new_items[rows] = now - item_step * (grad + shrinkage * now)
+        return carry
+
+    lax.fori_loop(0, 32, item_finish, 0)
+    for m in range(1, 8):
+        mid_grad_copy(m).wait_recv()
     for m in range(1, 8):
         grad_copy(m).wait_recv()
 
     def user_finish(j, carry):
-        grad = decode(grads.at[j])
+        grad = jnp.concatenate(
+            [decode(grads.at[j], 2 * EDGE_ROWS), decode(mid_grads.at[j], MIDDLE_ROWS)], axis=0
+        )
         rows = pl.ds(pl.multiple_of(j * 128, 128), 128)
         now = own_users[rows].astype(jnp.float32)
         new_users[rows] = now - user_step * (grad + shrinkage * now)
@@ -671,17 +785,27 @@
     lax.fori_loop(0, 8, user_finish, 0)
     for m in range(1, 8):
         grad_copy(m).wait_send()
+    for early in (item_first, item_pair, item_share, item_last):
+        early.wait_send()
 
 
 def reduce(sums, item_sums, own_users, own_items):
     vmem = pl.BlockSpec(memory_space=pltpu.VMEM)
     dma = pltpu.SemaphoreType.DMA
     i16, f32 = jnp.int16, jnp.float32
-    half = (2, 8, 2, 128 + SCALE_ROWS, 128)
-    near = (2, 8, 2, 256 + SCALE_ROWS, 128)
-    far = (2, 2, 128 + SCALE_ROWS, 128)
-    column = (2, 3, 2, 256 + SCALE_ROWS, 128)
-    last = (2, 3, 64 + SCALE_ROWS, 128)
+    half = (2, 8, 2, coded_rows(CHUNK // 2), 128)
+    near = (2, 8, 2, coded_rows(CHUNK), 128)
+    far = (2, 2, coded_rows(CHUNK // 2), 128)
+    column = (2, 3, 2, coded_rows(CHUNK), 128)
+    last = (2, 3, coded_rows(EDGE_ROWS), 128)
+    mid_far = (2, coded_rows(8 * MIDDLE_ROWS), 128)
+    mid = (3, 2, coded_rows(16 * MIDDLE_ROWS), 128)
+    mid_y = (3, coded_rows(4 * MIDDLE_ROWS), 128)
+    mid_x = (3, coded_rows(MIDDLE_ROWS), 128)
+    item_z = (7, coded_rows(32), 128)
+    item_pair = (coded_rows(256), 128)
+    both = lambda shape: [pltpu.VMEM(shape, i16)] * 2
+    sems = lambda *shape: [dma(shape)] * 2
     return pl.pallas_call(
         reduce_kernel,
         out_shape=(
@@ -691,21 +815,25 @@
         in_specs=[vmem, vmem, vmem, vmem],
         out_specs=(vmem, vmem),
         scratch_shapes=[
-            pltpu.VMEM(half, i16), pltpu.VMEM(half, i16),
-            pltpu.VMEM(near, i16), pltpu.VMEM(near, i16),
-            pltpu.VMEM(far, i16), pltpu.VMEM(far, i16),
-            pltpu.VMEM(column, i16), pltpu.VMEM(column, i16),
-            pltpu.VMEM((2, 2, 256, 128), f32),
-            pltpu.VMEM(last, i16), pltpu.VMEM(last, i16),
-            pltpu.VMEM((8, 128 + SCALE_ROWS, 128), i16),
+            *both(half), *both(near), *both(far), *both(column),
+            pltpu.VMEM((2, 2, CHUNK, 128), f32),
+            *both(last),
+            pltpu.VMEM((8, coded_rows(2 * EDGE_ROWS), 128), i16),
+            *both(mid_far), *both(mid),
+            pltpu.VMEM((16 * MIDDLE_ROWS, 128), f32),
+            *both(mid_y),
+            pltpu.VMEM((4 * MIDDLE_ROWS, 128), f32),
+            *both(mid_x),
+            pltpu.VMEM((8, coded_rows(MIDDLE_ROWS), 128), i16),
             pltpu.VMEM((4, 128, 128), f32), pltpu.VMEM((512, 128), f32),
-            pltpu.VMEM((7, 64 + SCALE_ROWS, 128), i16), pltpu.VMEM((7, 64 + SCALE_ROWS, 128), i16),
-            pltpu.VMEM((64, 128), f32), pltpu.VMEM((32, 128), f32),
-            pltpu.VMEM((2, 8, 2, 32 + SCALE_ROWS, 128), i16),
-            dma((2, 8, 2)), dma((2, 8, 2)), dma((2, 8, 2)), dma((2, 8, 2)),
-            dma((2, 2)), dma((2, 2)), dma((2, 3, 2)), dma((2, 3, 2)),
-            dma((2, 3)), dma((2, 3)), dma((7,)), dma((7,)),
-            dma((4,)), dma((4,)), dma((7,)), dma((7,)), dma((7,)), dma((7,)),
+            *both(item_pair),
+            pltpu.VMEM((256, 128), f32),
+            *both(item_z),
+            pltpu.VMEM((2, 2, 8, coded_rows(32), 128), i16),
+            *sems(2, 8, 2), *sems(2, 8, 2), *sems(2, 2), *sems(2, 3, 2),
+            *sems(2, 3), *sems(7),
+            *sems(2), *sems(3, 2), *sems(3), *sems(3), *sems(7),
+            *sems(4), *sems(7), *sems(7),
         ],
         compiler_params=pltpu.CompilerParams(
             collective_id=1, has_side_effects=True, vmem_limit_bytes=16 * 2**20

time: 93.9 us -> 88.7 us (0.945); the launches traced: 93.8 us -> 87.7 us
  Pallas kernels: 90 us -> 83.8 us
    pallas_call x1, Pallas kernels: 52.5 us -> 46.3 us  [reduce(): pl.pallas_call(reduce_kernel, out_shape=(jax.ShapeDtypeStruct((1024, 128)...]
where the time goes in v4:
time: 88.7 us; the launch traced here: 87.7 us
  Pallas kernels  83.8 us (94%)
  local copies, waits for them, and re-layouts  1.75 us (2%)
  between operations  1.38 us (2%)
    pallas_call x1, Pallas kernels, reduce(): pl.pallas_call(reduce_kernel, out_shape=(jax.ShapeDtypeStruct((1024, 128)...  46.3 us
    pallas_call x1, Pallas kernels, gather(): pl.pallas_call(functools.partial(gather_kernel, (ROWS_A, ROWS_B, ROWS_C))...  34.2 us
    pallas_call x1, Pallas kernels, local(): pl.pallas_call(local_kernel, out_shape=(jax.ShapeDtypeStruct((128, 128, 1...  3.27 us

profile of v4, /device:TPU:6, one launch (start us, length us, event | category | flops | bytes accessed | tf_op | source)
XLA Modules:
  0.0 87.7 jit_solution(5837598307457493816)
XLA Ops:
  0.6 0.0 copy-start
  1.3 0.1 pad.2.clone
  1.4 0.1 pad.3.clone
  1.5 0.7 add_add_fusion.lists
  2.2 34.2 %shard_map.77 = (bf16[8,2,2,4,128,128]{5,4,3,2,1,0:T(8,128)(2,1)S(1)}, s32[2,128,128,128]{3,2,1,0:T(8,128)S(1)}, s32[2,8,128]{2,1,0:T(8,128)S(1)}, f32[128,128,128]{2,1,0:T(8,128)S(1)}, f32[8,128,128]{2,1,0:T(8,128)S(1)}) custom-call(bf16[2,4,128,128]{3,2,1,0:T(8,128)(2,1)} %bitcast.17, s32[128,128,128]{2,1,0:T(8,128)} %bitcast.18, ...), custom_call_target="tpu_custom_call" | custom-call | tf_op jit(solution)/shard_map/pallas_call | solution.py:238
  36.4 0.0 copy-done
  36.4 0.0 copy-start.1
  36.5 3.3 %shard_map.78 = (f32[128,128,128]{2,1,0:T(8,128)S(1)}, f32[8,128,128]{2,1,0:T(8,128)S(1)}) custom-call(s32[1]{0:T(128)} %bitcast.core, s32[2,8,128]{2,1,0:T(8,128)S(1)} %get-tuple-element.9.lists, bf16[128,128,128]{2,1,0:T(8,128)(2,1)S(1)} %bitcast.15, bf16[8,128,128]{2,1,0:T(8,128)(2,1)S(1)} %bitcast.16, ...), custom_call_target="tpu_custom_call", output_to_operand_aliasing={{0}: (5, {}), {1}: (6, {})} | custom-call | tf_op jit(solution)/shard_map/pallas_call | solution.py:331
  39.7 0.0 copy-done.1
  39.8 46.3 %shard_map.79 = (f32[1024,128]{1,0:T(8,128)S(1)}, f32[1024,128]{1,0:T(8,128)S(1)}) custom-call(f32[8,2,2,4,128,128]{5,4,3,2,1,0:T(8,128)S(1)} %bitcast.13, f32[8,128,128]{2,1,0:T(8,128)S(1)} %get-tuple-element.15.item_sums, bf16[1024,128]{1,0:T(8,128)(2,1)S(1)} %copy-done.1, bf16[1024,128]{1,0:T(8,128)(2,1)S(1)} %copy-done), custom_call_target="tpu_custom_call" | custom-call | tf_op jit(solution)/shard_map/pallas_call | solution.py:809
  86.1 0.8 copy.15
  86.9 0.8 copy.16
  (1 shorter events, 0.0 us)
Async XLA Ops:
  0.6 35.8 %copy-start = (bf16[1024,128]{1,0:T(8,128)(2,1)S(1)}, bf16[1024,128]{1,0:T(8,128)(2,1)}, u32[]{:S(2)}) copy-start(bf16[1024,128]{1,0:T(8,128)(2,1)} %own_items.1) | copy-start | bytes 786436
  36.4 3.3 %copy-start.1 = (bf16[1024,128]{1,0:T(8,128)(2,1)S(1)}, bf16[1024,128]{1,0:T(8,128)(2,1)}, u32[]{:S(2)}) copy-start(bf16[1024,128]{1,0:T(8,128)(2,1)} %own_users.1) | copy-start | bytes 786436

commit v5 on v4

--- a/solution.py
+++ b/solution.py
@@ -278,15 +278,20 @@
     mine = core[0]
 
     def scan(table):
-        def visit(slot, count):
-            block = lists[table, 0, slot]
-            order[count] = ((table * 128 + slot) * 256 + block) * 8 + lists[table, 1, slot]
-            keep = lax.rem(block // 8, 2) == mine
-            return count + keep.astype(jnp.int32)
-        return visit
-
-    count = lax.fori_loop(0, lists[0, 2, 0], scan(0), jnp.int32(0))
-    count = lax.fori_loop(0, lists[1, 2, 0], scan(1), count)
+        live = lists[table, 2, 0]
+
+        def visit(eight, count):
+            for k in range(8):
+                slot = eight * 8 + k
+                block = lists[table, 0, slot]
+                order[count] = ((table * 128 + slot) << 11) | (block << 3) | lists[table, 1, slot]
+                keep = (((block >> 3) & 1) == mine) & (slot < live)
+                count = count + keep.astype(jnp.int32)
+            return count
+
+        return lambda count: lax.fori_loop(0, (live + 7) >> 3, visit, count)
+
+    count = scan(1)(scan(0)(jnp.int32(0)))
     for k in range(GROUP):
         order[count + k] = 0
 
@@ -296,15 +301,14 @@
         for k in range(GROUP):
             n = first + k
             entry = order[n]
-            item = lax.rem(entry, 8)
-            block = lax.rem(entry // 8, 256)
-            tile = (block // 16) * 8 + lax.rem(block, 8)
+            item = entry & 7
+            tile = ((entry >> 7) & 15) * 8 + ((entry >> 3) & 7)
             user_tile = users[tile]
             item_tile = items[item]
             predicted = lax.dot_general(
                 user_tile, item_tile, (((1,), (1,)), ((), ())), preferred_element_type=jnp.float32
             )
-            scores = ratings[entry // 2048]
+            scores = ratings[entry >> 11]
             floor = jnp.where(n < count, 0, 1 << 20)
             errors = jnp.where(
                 scores > floor, predicted - (scores.astype(jnp.float32) - 3.0), 0.0

time: 88.7 us -> 87.5 us (0.986)
  Pallas kernels: 83.8 us -> 82.7 us
    pallas_call x1, Pallas kernels: 46.3 us -> 44.5 us  [reduce(): pl.pallas_call(reduce_kernel, out_shape=(jax.ShapeDtypeStruct((1024, 128)...]
where the time goes in v5:
time: 87.5 us; the launch traced here: 86.6 us
  Pallas kernels  82.7 us (95%)
  local copies, waits for them, and re-layouts  1.75 us (2%)
  between operations  1.38 us (2%)
    pallas_call x1, Pallas kernels, reduce(): pl.pallas_call(reduce_kernel, out_shape=(jax.ShapeDtypeStruct((1024, 128)...  44.5 us
    pallas_call x1, Pallas kernels, gather(): pl.pallas_call(functools.partial(gather_kernel, (ROWS_A, ROWS_B, ROWS_C))...  34.2 us
    pallas_call x1, Pallas kernels, local(): pl.pallas_call(local_kernel, out_shape=(jax.ShapeDtypeStruct((128, 128, 1...  4.06 us

profile of v5, /device:TPU:6, one launch (start us, length us, event | category | flops | bytes accessed | tf_op | source)
XLA Modules:
  0.0 86.6 jit_solution(7092434570084101680)
XLA Ops:
  0.6 0.0 copy-start
  1.3 0.1 pad.2.clone
  1.4 0.1 pad.3.clone
  1.5 0.7 add_add_fusion.lists
  2.2 34.2 %shard_map.77 = (bf16[8,2,2,4,128,128]{5,4,3,2,1,0:T(8,128)(2,1)S(1)}, s32[2,128,128,128]{3,2,1,0:T(8,128)S(1)}, s32[2,8,128]{2,1,0:T(8,128)S(1)}, f32[128,128,128]{2,1,0:T(8,128)S(1)}, f32[8,128,128]{2,1,0:T(8,128)S(1)}) custom-call(bf16[2,4,128,128]{3,2,1,0:T(8,128)(2,1)} %bitcast.17, s32[128,128,128]{2,1,0:T(8,128)} %bitcast.18, ...), custom_call_target="tpu_custom_call" | custom-call | tf_op jit(solution)/shard_map/pallas_call | solution.py:238
  36.4 0.0 copy-done
  36.4 0.0 copy-start.1
  36.5 4.1 %shard_map.78 = (f32[128,128,128]{2,1,0:T(8,128)S(1)}, f32[8,128,128]{2,1,0:T(8,128)S(1)}) custom-call(s32[1]{0:T(128)} %bitcast.core, s32[2,8,128]{2,1,0:T(8,128)S(1)} %get-tuple-element.9.lists, bf16[128,128,128]{2,1,0:T(8,128)(2,1)S(1)} %bitcast.15, bf16[8,128,128]{2,1,0:T(8,128)(2,1)S(1)} %bitcast.16, ...), custom_call_target="tpu_custom_call", output_to_operand_aliasing={{0}: (5, {}), {1}: (6, {})} | custom-call | tf_op jit(solution)/shard_map/pallas_call | solution.py:335
  40.5 0.0 copy-done.1
  40.5 44.5 %shard_map.79 = (f32[1024,128]{1,0:T(8,128)S(1)}, f32[1024,128]{1,0:T(8,128)S(1)}) custom-call(f32[8,2,2,4,128,128]{5,4,3,2,1,0:T(8,128)S(1)} %bitcast.13, f32[8,128,128]{2,1,0:T(8,128)S(1)} %get-tuple-element.15.item_sums, bf16[1024,128]{1,0:T(8,128)(2,1)S(1)} %copy-done.1, bf16[1024,128]{1,0:T(8,128)(2,1)S(1)} %copy-done), custom_call_target="tpu_custom_call" | custom-call | tf_op jit(solution)/shard_map/pallas_call | solution.py:813
  85.0 0.8 copy.15
  85.8 0.8 copy.16
  (1 shorter events, 0.0 us)
Async XLA Ops:
  0.6 35.8 %copy-start = (bf16[1024,128]{1,0:T(8,128)(2,1)S(1)}, bf16[1024,128]{1,0:T(8,128)(2,1)}, u32[]{:S(2)}) copy-start(bf16[1024,128]{1,0:T(8,128)(2,1)} %own_items.1) | copy-start | bytes 786436
  36.4 4.1 %copy-start.1 = (bf16[1024,128]{1,0:T(8,128)(2,1)S(1)}, bf16[1024,128]{1,0:T(8,128)(2,1)}, u32[]{:S(2)}) copy-start(bf16[1024,128]{1,0:T(8,128)(2,1)} %own_users.1) | copy-start | bytes 786436

commit v6 on v5

--- a/solution.py
+++ b/solution.py
@@ -145,7 +145,7 @@
         first["x", offset, low] = [send(block, block, near["x"][way]) for way in (0, 1)]
 
     def y_send(offset):
-        if offset in late:
+        if offset == 4:
             block = part_b(zed(offset), y)
             for k in (2, 1, 3):
                 direct(block, device(z, lax.rem(y + k, 4), x, c))
@@ -155,7 +155,7 @@
 
     def forward(axis, offset, low):
         zz = zed(offset)
-        if axis == "x" and offset == 0 and low == 0 or offset in late:
+        if axis == "x" and (offset == 0 and low == 0 or offset in late) or offset == 4:
             return
         for way in (0, 1):
             first[axis, offset, low][way].wait_recv()

time: 87.5 us -> 87.7 us (level)
  Pallas kernels: 82.7 us -> 83.8 us
    pallas_call x1, Pallas kernels: 44.5 us -> 47.3 us  [reduce(): pl.pallas_call(reduce_kernel, out_shape=(jax.ShapeDtypeStruct((1024, 128)...]
    pallas_call x1, Pallas kernels: 4.06 us -> 2.93 us  [local(): pl.pallas_call(local_kernel, out_shape=(jax.ShapeDtypeStruct((128, 128, 1...]
where the time goes in v6:
time: 87.7 us
  Pallas kernels  83.8 us (96%)
  local copies, waits for them, and re-layouts  1.75 us (2%)
  between operations  1.38 us (2%)
    pallas_call x1, Pallas kernels, reduce(): pl.pallas_call(reduce_kernel, out_shape=(jax.ShapeDtypeStruct((1024, 128)...  47.3 us
    pallas_call x1, Pallas kernels, gather(): pl.pallas_call(functools.partial(gather_kernel, (ROWS_A, ROWS_B, ROWS_C))...  33.6 us
    pallas_call x1, Pallas kernels, local(): pl.pallas_call(local_kernel, out_shape=(jax.ShapeDtypeStruct((128, 128, 1...  2.93 us

profile of v6, /device:TPU:6, one launch (start us, length us, event | category | flops | bytes accessed | tf_op | source)
XLA Modules:
  0.0 87.7 jit_solution(9700054914409824690)
XLA Ops:
  0.6 0.0 copy-start
  1.3 0.1 pad.2.clone
  1.4 0.1 pad.3.clone
  1.5 0.7 add_add_fusion.lists
  2.2 33.6 %shard_map.77 = (bf16[8,2,2,4,128,128]{5,4,3,2,1,0:T(8,128)(2,1)S(1)}, s32[2,128,128,128]{3,2,1,0:T(8,128)S(1)}, s32[2,8,128]{2,1,0:T(8,128)S(1)}, f32[128,128,128]{2,1,0:T(8,128)S(1)}, f32[8,128,128]{2,1,0:T(8,128)S(1)}) custom-call(bf16[2,4,128,128]{3,2,1,0:T(8,128)(2,1)} %bitcast.17, s32[128,128,128]{2,1,0:T(8,128)} %bitcast.18, ...), custom_call_target="tpu_custom_call" | custom-call | tf_op jit(solution)/shard_map/pallas_call | solution.py:238
  35.8 0.0 copy-done
  35.8 0.0 copy-start.1
  35.8 2.9 %shard_map.78 = (f32[128,128,128]{2,1,0:T(8,128)S(1)}, f32[8,128,128]{2,1,0:T(8,128)S(1)}) custom-call(s32[1]{0:T(128)} %bitcast.core, s32[2,8,128]{2,1,0:T(8,128)S(1)} %get-tuple-element.9.lists, bf16[128,128,128]{2,1,0:T(8,128)(2,1)S(1)} %bitcast.15, bf16[8,128,128]{2,1,0:T(8,128)(2,1)S(1)} %bitcast.16, ...), custom_call_target="tpu_custom_call", output_to_operand_aliasing={{0}: (5, {}), {1}: (6, {})} | custom-call | tf_op jit(solution)/shard_map/pallas_call | solution.py:335
  38.8 0.0 copy-done.1
  38.8 47.3 %shard_map.79 = (f32[1024,128]{1,0:T(8,128)S(1)}, f32[1024,128]{1,0:T(8,128)S(1)}) custom-call(f32[8,2,2,4,128,128]{5,4,3,2,1,0:T(8,128)S(1)} %bitcast.13, f32[8,128,128]{2,1,0:T(8,128)S(1)} %get-tuple-element.15.item_sums, bf16[1024,128]{1,0:T(8,128)(2,1)S(1)} %copy-done.1, bf16[1024,128]{1,0:T(8,128)(2,1)S(1)} %copy-done), custom_call_target="tpu_custom_call" | custom-call | tf_op jit(solution)/shard_map/pallas_call | solution.py:813
  86.1 0.8 copy.15
  86.9 0.8 copy.16
  (1 shorter events, 0.0 us)
Async XLA Ops:
  0.6 35.2 %copy-start = (bf16[1024,128]{1,0:T(8,128)(2,1)S(1)}, bf16[1024,128]{1,0:T(8,128)(2,1)}, u32[]{:S(2)}) copy-start(bf16[1024,128]{1,0:T(8,128)(2,1)} %own_items.1) | copy-start | bytes 786436
  35.8 2.9 %copy-start.1 = (bf16[1024,128]{1,0:T(8,128)(2,1)S(1)}, bf16[1024,128]{1,0:T(8,128)(2,1)}, u32[]{:S(2)}) copy-start(bf16[1024,128]{1,0:T(8,128)(2,1)} %own_users.1) | copy-start | bytes 786436
